TPU v7x, 128 devices: a whole 4x4x4 slice. The times are simulated.
128 devices in a mesh: wall: 8 (over x, core), pen: 16 (over z, y).
Axes of the slice: x: 4, y: 4, z: 4, core: 2. Of those that a mesh axis runs over, the one named last changes fastest.
Arguments:
- right_side: float32 [32, 2048, 1024], P('wall', 'pen'), may hold values from -48 to 48
- coef_table: float32 [64, 3], replicated, may hold values from 0.25 to 16, as said below
- stretch_index: int32 [32], replicated, may hold values from 0 to 63
- stream_wave: int32 [512], replicated, may hold values from 0 to 1023
- span_wave: int32 [2048], replicated, may hold values from 0 to 2047
Outputs:
- pressure: float32 [32, 2048, 1024], P('wall', 'pen')
Inputs may be any that keep to these rules, and one draw needn't show every extreme that they name: `coef_table`: all entries positive.
All inputs are finite; a program needn't handle non-finite values.
Results may differ from a plain program's by a relative error of at most 0.00018.
Values sent between devices are 32-bit elements; how exact they have to be, the bound alone decides.
No kernel may reach another device: no remote copies, remote signals or barrier semaphores. Data moves between devices by JAX's collectives and lax.ppermute only.
A program may use at most 192 MiB of HBM per device.

v0:
```python
import jax
import jax.numpy as jnp
from jax import lax
from jax.sharding import PartitionSpec as P

HIGHEST = lax.Precision.HIGHEST


def shifted(block, axis, distance):
    devices = range(lax.axis_size(axis))
    route = [(i - distance, i) for i in devices if i - distance in devices]
    return lax.ppermute(block, axis, route)


def angle_pair(rows, cols, length):
    row_ids = jnp.arange(rows, dtype=jnp.int32)[:, None]
    col_ids = jnp.arange(cols, dtype=jnp.int32)[None, :]
    angle = (row_ids * col_ids % length).astype(jnp.float32) * (2.0 * jnp.pi / length)
    return (jnp.cos(angle), jnp.sin(angle))


def factor_tables(length):
    first = 32
    second = length // first
    inner_cos, inner_sin = angle_pair(second, second, second)
    twist_cos, twist_sin = angle_pair(second, first, length)
    outer_cos, outer_sin = angle_pair(first, first, first)
    return (inner_cos, inner_sin, twist_cos, twist_sin, outer_cos, outer_sin)


def factored_dft(real_part, imag_part, tables, sign):
    inner_cos, inner_sin, twist_cos, twist_sin, outer_cos, outer_sin = tables
    second = inner_cos.shape[0]
    first = outer_cos.shape[0]
    leading = real_part.shape[:-1]
    length = real_part.shape[-1]
    real_grid = real_part.reshape(leading + (second, first))
    imag_grid = imag_part.reshape(leading + (second, first))
    real_cos = jnp.einsum("...uv,uw->...wv", real_grid, inner_cos, precision=HIGHEST)
    real_sin = jnp.einsum("...uv,uw->...wv", real_grid, inner_sin, precision=HIGHEST)
    imag_cos = jnp.einsum("...uv,uw->...wv", imag_grid, inner_cos, precision=HIGHEST)
    imag_sin = jnp.einsum("...uv,uw->...wv", imag_grid, inner_sin, precision=HIGHEST)
    section_real = real_cos - sign * imag_sin
    section_imag = imag_cos + sign * real_sin
    turned_real = section_real * twist_cos - sign * section_imag * twist_sin
    turned_imag = section_imag * twist_cos + sign * section_real * twist_sin
    real_cos = jnp.einsum("...wv,vm->...mw", turned_real, outer_cos, precision=HIGHEST)
    real_sin = jnp.einsum("...wv,vm->...mw", turned_real, outer_sin, precision=HIGHEST)
    imag_cos = jnp.einsum("...wv,vm->...mw", turned_imag, outer_cos, precision=HIGHEST)
    imag_sin = jnp.einsum("...wv,vm->...mw", turned_imag, outer_sin, precision=HIGHEST)
    out_real = (real_cos - sign * imag_sin).reshape(leading + (length,))
    out_imag = (imag_cos + sign * real_sin).reshape(leading + (length,))
    return (out_real, out_imag)


def modified_wave(indices, length):
    return (2.0 * jnp.sin(jnp.pi * indices.astype(jnp.float32) / length)) ** 2


def chain_solve(lower_band, middle_band, upper_band, source):
    count = source.shape[0]
    ratios = []
    partial_value = []
    for position in range(count):
        if position == 0:
            divisor = middle_band[0]
            partial_value.append(source[0] / divisor)
        else:
            divisor = middle_band[position] - lower_band[position] * ratios[-1]
            partial_value.append(
                (source[position] - lower_band[position] * partial_value[-1]) / divisor
            )
        ratios.append(upper_band[position] / divisor)
    solved = [partial_value[count - 1]]
    for position in range(count - 2, -1, -1):
        solved.insert(0, partial_value[position] - ratios[position] * solved[0])
    return jnp.stack(solved, axis=0)


def on_device(right_side, coef_table, stretch_index, stream_wave, span_wave):
    planes = right_side.shape[0]
    length_x = right_side.shape[2]
    length_z = span_wave.shape[0]
    modes_x = length_x // 2
    pen_count = lax.axis_size("pen")
    pen_index = lax.axis_index("pen")
    wall_index = lax.axis_index("wall")
    modes_local = modes_x // pen_count
    tables_x = factor_tables(length_x)
    tables_z = factor_tables(length_z)
    weights = jnp.where(jnp.arange(modes_x) == 0, 1.0, 2.0).astype(jnp.float32) / (
        length_x * length_z
    )
    stream_real, stream_imag = factored_dft(right_side, jnp.zeros_like(right_side), tables_x, -1.0)
    stream_real = stream_real[:, :, :modes_x]
    stream_imag = stream_imag[:, :, :modes_x]
    wave_z = modified_wave(span_wave, length_z)
    levels = coef_table.shape[0]
    onehot = (stretch_index[:, None] == jnp.arange(levels, dtype=jnp.int32)[None, :]).astype(
        jnp.float32
    )
    profile = jnp.dot(onehot, coef_table, precision=HIGHEST)
    spectral = jnp.transpose(jnp.stack([stream_real, stream_imag], axis=1), (0, 1, 3, 2))
    block = lax.all_to_all(spectral, "pen", split_axis=2, concat_axis=3, tiled=True)
    out_real, out_imag = factored_dft(block[:, 0], block[:, 1], tables_z, -1.0)
    spectrum = jnp.stack([out_real, out_imag], axis=1)
    wave_x = modified_wave(
        lax.dynamic_slice_in_dim(stream_wave, pen_index * modes_local, modes_local), length_x
    )
    squared = wave_x[:, None] + wave_z[None, :]
    local_rows = lax.dynamic_slice_in_dim(profile, wall_index * planes, planes, 0)
    lower_row = local_rows[:, 0]
    upper_row = local_rows[:, 1]
    middle = -(lower_row + upper_row + local_rows[:, 2])[:, None, None] - squared[None]
    interior = planes - 1
    ratios = []
    down_f = []
    down_u = []
    for position in range(interior):
        if position == 0:
            divisor = middle[0]
            down_f.append(spectrum[0] / divisor)
            down_u.append(-lower_row[0] / divisor)
        else:
            divisor = middle[position] - lower_row[position] * ratios[-1]
            down_f.append((spectrum[position] - lower_row[position] * down_f[-1]) / divisor)
            down_u.append(-lower_row[position] * down_u[-1] / divisor)
        ratios.append(upper_row[position] / divisor)
        if position == interior - 1:
            last_w = -upper_row[position] / divisor
    part_f = [down_f[interior - 1]]
    part_u = [down_u[interior - 1]]
    part_w = [last_w]
    for position in range(interior - 2, -1, -1):
        part_f.insert(0, down_f[position] - ratios[position] * part_f[0])
        part_u.insert(0, down_u[position] - ratios[position] * part_u[0])
        part_w.insert(0, -ratios[position] * part_w[0])
    next_f, next_u, next_w = shifted((part_f[0], part_u[0], part_w[0]), "wall", -1)
    edge_lower = lower_row[interior]
    edge_upper = upper_row[interior]
    red_lower = edge_lower * part_u[-1]
    red_middle = edge_lower * part_w[-1] + middle[interior] + edge_upper * next_u
    red_upper = edge_upper * next_w
    red_source = spectrum[interior] - edge_lower * part_f[-1] - edge_upper * next_f
    received = (
        lax.all_to_all(red_lower[None, None], "wall", split_axis=3, concat_axis=0, tiled=True),
        lax.all_to_all(red_middle[None, None], "wall", split_axis=3, concat_axis=0, tiled=True),
        lax.all_to_all(red_upper[None, None], "wall", split_axis=3, concat_axis=0, tiled=True),
        lax.all_to_all(red_source[None], "wall", split_axis=3, concat_axis=0, tiled=True),
    )
    chain_values = chain_solve(received[0], received[1], received[2], received[3])
    padded = jnp.concatenate([jnp.zeros_like(chain_values[:1]), chain_values], axis=0)
    pair_values = jnp.stack([padded[:-1], padded[1:]], axis=1)
    returned_pairs = lax.all_to_all(pair_values, "wall", split_axis=0, concat_axis=4, tiled=True)
    left_value = returned_pairs[0, 0]
    own_value = returned_pairs[0, 1]
    rows_out = [
        part_f[position] + part_u[position] * left_value + part_w[position] * own_value
        for position in range(interior)
    ]
    rows_out.append(own_value)
    solved = jnp.stack(rows_out, axis=0)
    out_real, out_imag = factored_dft(solved[:, 0], solved[:, 1], tables_z, 1.0)
    back_spectrum = jnp.stack([out_real, out_imag], axis=1)
    returned = lax.all_to_all(back_spectrum, "pen", split_axis=3, concat_axis=2, tiled=True)
    padding = ((0, 0), (0, 0), (0, length_x - modes_x))
    full_real = jnp.pad(jnp.transpose(returned[:, 0], (0, 2, 1)) * weights, padding)
    full_imag = jnp.pad(jnp.transpose(returned[:, 1], (0, 2, 1)) * weights, padding)
    out_real, _ = factored_dft(full_real, full_imag, tables_x, 1.0)
    return out_real


def solution(mesh):
    in_specs = (P("wall", "pen", None), P(), P(), P(), P())
    out_specs = P("wall", "pen", None)
    return jax.shard_map(
        on_device, mesh=mesh, in_specs=in_specs, out_specs=out_specs, check_vma=False
    )
```

profile of v0, /device:TPU:1, one launch (start us, length us, event | category | flops | bytes accessed | tf_op | source)
XLA Modules:
  0.0 490.2 jit_solution(14340683255911169025)
XLA Ops:
  15.6 9.3 %reduce.2 = f32[2048,32]{1,0:T(8,128)S(1)} reduce(f32[2048,1,1,32]{3,2,1,0:T(1,128)S(1)} %bitcast.583, f32[]{:T(128)} %broadcast.1264), dimensions={1,2}, to_apply=%bitcast.492.reduce_sub_computation | reduce | bytes 524292
  26.0 5.8 %all-to-all-start.4 = ((f32[8,1,8192]{2,1,0:T(1,128)}), f32[8,1,8192]{2,1,0:T(1,128)}, u32[]{:S(2)}, u32[]{:S(2)}) async-start(f32[8,1,8192]{2,1,0:T(1,128)} %reshape.1374), calls=%async_computation.4 | async-start | bytes 524288 | tf_op jit(solution)/shard_map/all_to_all | solution.py:146
  65.5 7.8 %all-to-all-start = ((f32[4,2,512,128]{3,0,1,2:T(4,128)}), f32[4,2,512,128]{3,0,1,2:T(4,128)S(1)}, u32[]{:S(2)}, u32[]{:S(2)}) async-start(f32[4,2,512,128]{3,0,1,2:T(4,128)} %copy.262), calls=%async_computation | async-start | bytes 4194304 | tf_op jit(solution)/shard_map/all_to_all | solution.py:104
  97.7 10.3 %reduce = f32[2048,32]{1,0:T(8,128)} reduce(f32[2048,1,1,32]{3,2,1,0:T(1,128)S(1)} %bitcast.584, f32[]{:T(128)} %broadcast.1264), dimensions={1,2}, to_apply=%bitcast.488.reduce_sub_computation | reduce | bytes 524292
  110.3 6.1 %all-to-all-start.2 = ((f32[8,1,8192]{2,1,0:T(1,128)}), f32[8,1,8192]{2,1,0:T(1,128)}, u32[]{:S(2)}, u32[]{:S(2)}) async-start(f32[8,1,8192]{2,1,0:T(1,128)} %reshape.1370), calls=%async_computation.2 | async-start | bytes 524288 | tf_op jit(solution)/shard_map/all_to_all | solution.py:147
  120.1 9.4 %fusion.127 = f32[64,4,32,32]{0,3,2,1:T(8,128)} fusion(f32[4,32,64,32]{3,2,1,0:T(8,128)} %reshape_squeeze.13), kind=kOutput, calls=%fused_computation.234 | convolution fusion | flops 201383936 | bytes 2097152 | tf_op jit(solution)/shard_map/...uv,uw->...wv/dot_general | solution.py:41
  132.3 8.9 %fusion.129 = f32[64,4,32,32]{0,3,2,1:T(8,128)S(1)} fusion(f32[4,32,64,32]{3,2,1,0:T(8,128)} %reshape_squeeze.12), kind=kOutput, calls=%fused_computation.236 | convolution fusion | flops 201383936 | bytes 2097152 | tf_op jit(solution)/shard_map/...uv,uw->...wv/dot_general | solution.py:39
  141.2 6.8 %multiply_add_fusion.2 = f32[64,4,32,32]{0,3,2,1:T(8,128)S(1)} fusion(f32[64,4,32,32]{0,3,2,1:T(8,128)S(1)} %copy-done.9, f32[4,32,64,32]{3,2,1,0:T(8,128)S(1)} %copy-done.6), kind=kOutput, calls=%fused_computation.41 | convolution fusion | flops 201908224 | bytes 3145728 | tf_op jit(solution)/shard_map/...uv,uw->...wv/dot_general | solution.py:40
  148.0 6.9 %multiply_subtract_fusion.2 = f32[64,4,32,32]{0,3,2,1:T(8,128)S(1)} fusion(f32[64,4,32,32]{0,3,2,1:T(8,128)S(1)} %fusion.129, f32[4,32,64,32]{3,2,1,0:T(8,128)S(1)} %copy-done.4), kind=kOutput, calls=%fused_computation.42 | convolution fusion | flops 201908224 | bytes 3145728 | tf_op jit(solution)/shard_map/...uv,uw->...wv/dot_general | solution.py:42
  165.8 5.7 %add_bitcast_fusion.2 = f32[4,32,32,64]{3,2,1,0:T(8,128)} fusion(f32[32,4,32,64]{3,0,2,1:T(8,128)} %fusion.8, f32[64,4,32,32]{0,3,2,1:T(8,128)S(1)} %multiply_add_fusion.2, f32[64,4,32,32]{0,3,2,1:T(8,128)} %copy-done.2, f32[64,32]{0,1:T(8,128)S(1)} %get-tuple-element.93, f32[64,32]{0,1:T(8,128)S(1)} %get-tuple-element.94), kind=kOutput, calls=%fused_computation.37 | convolution fusion | flops 101988352 | bytes 4210688 | tf_op jit(solution)/shard_map/...wv,vm->...mw/dot_general | solution.py:48
  183.1 11.3 %reduce.4 = f32[2048,32]{1,0:T(8,128)} reduce(f32[2048,1,1,32]{3,2,1,0:T(1,128)} %bitcast.585, f32[]{:T(128)} %broadcast.1264), dimensions={1,2}, to_apply=%bitcast.490.reduce_sub_computation | reduce | bytes 524292
  283.3 15.0 %all-to-all-done.5 = f32[8,2,2,32,256]{4,3,2,1,0:T(8,128)S(1)} async-done(((f32[8,2,2,32,256]{4,3,2,1,0:T(8,128)}), f32[8,2,2,32,256]{4,3,2,1,0:T(8,128)S(1)}, u32[]{:S(2)}, u32[]{:S(2)}) %all-to-all-start.5) | async-done | bytes 1048608 | tf_op jit(solution)/shard_map/all_to_all | solution.py:154
  308.3 9.4 %fusion.123 = f32[64,4,32,32]{0,3,2,1:T(8,128)} fusion(f32[4,32,64,32]{3,2,1,0:T(8,128)} %reshape_squeeze.15), kind=kOutput, calls=%fused_computation.230 | convolution fusion | flops 201383936 | bytes 2097152 | tf_op jit(solution)/shard_map/...uv,uw->...wv/dot_general | solution.py:41
  320.5 9.1 %fusion.125 = f32[64,4,32,32]{0,3,2,1:T(8,128)S(1)} fusion(f32[4,32,64,32]{3,2,1,0:T(8,128)} %reshape_squeeze.14), kind=kOutput, calls=%fused_computation.232 | convolution fusion | flops 201383936 | bytes 2097152 | tf_op jit(solution)/shard_map/...uv,uw->...wv/dot_general | solution.py:39
  329.6 6.8 %convolution_add_fusion = f32[64,4,32,32]{0,3,2,1:T(8,128)S(1)} fusion(f32[64,4,32,32]{0,3,2,1:T(8,128)S(1)} %copy-done.10, f32[4,32,64,32]{3,2,1,0:T(8,128)S(1)} %copy-done.7), kind=kOutput, calls=%fused_computation.71 | convolution fusion | flops 201646080 | bytes 3145728 | tf_op jit(solution)/shard_map/...uv,uw->...wv/dot_general | solution.py:40
  336.4 6.8 %convolution_subtract_fusion = f32[64,4,32,32]{0,3,2,1:T(8,128)S(1)} fusion(f32[64,4,32,32]{0,3,2,1:T(8,128)S(1)} %fusion.125, f32[4,32,64,32]{3,2,1,0:T(8,128)S(1)} %copy-done.5), kind=kOutput, calls=%fused_computation.72 | convolution fusion | flops 201646080 | bytes 3145728 | tf_op jit(solution)/shard_map/...uv,uw->...wv/dot_general | solution.py:42
  367.3 11.8 %fusion.361 = f32[2048,4,2,32]{3,2,1,0:T(2,128)} fusion(f32[4,1,32,2048]{2,1,0,3:T(1,128)} %bitcast.552, f32[4,1,32,2048]{2,1,0,3:T(1,128)} %bitcast.551), kind=kLoop, calls=%fused_computation.438 | loop fusion | flops 524288 | bytes 4194304
  379.1 11.4 %reshape.1376 = f32[16,1,32768]{2,1,0:T(1,128)} reshape(f32[2048,4,2,32]{3,2,1,0:T(2,128)} %fusion.361) | data formatting | bytes 4194304
  390.5 6.8 %all-to-all-start.6 = ((f32[16,1,32768]{2,1,0:T(1,128)}), f32[16,1,32768]{2,1,0:T(1,128)}, u32[]{:S(2)}, u32[]{:S(2)}) async-start(f32[16,1,32768]{2,1,0:T(1,128)} %reshape.1376), calls=%async_computation.6 | async-start | bytes 4194304 | tf_op jit(solution)/shard_map/all_to_all | solution.py:165
  397.4 29.9 %all-to-all-done.6 = f32[16,1,32768]{2,1,0:T(1,128)} async-done(((f32[16,1,32768]{2,1,0:T(1,128)}), f32[16,1,32768]{2,1,0:T(1,128)}, u32[]{:S(2)}, u32[]{:S(2)}) %all-to-all-start.6) | async-done | bytes 2097184 | tf_op jit(solution)/shard_map/all_to_all | solution.py:165
  427.3 7.4 %reduce.7 = f32[16,32768]{1,0:T(8,128)S(1)} reduce(f32[16,1,32768]{2,1,0:T(1,128)} %all-to-all-done.6, f32[]{:T(128)} %broadcast.1264), dimensions={1}, to_apply=%all_to_all.103.reduce_sub_computation | reduce | bytes 4194308 | tf_op jit(solution)/shard_map/all_to_all | solution.py:165
  434.7 9.1 %reshape.1377 = f32[2048,4,2,32]{3,2,1,0:T(2,128)} reshape(f32[16,32768]{1,0:T(8,128)S(1)} %reduce.7) | data formatting | bytes 4194304
  443.8 10.2 %copy.341 = f32[4,2,32,16,128]{4,2,3,1,0:T(8,128)S(1)} copy(f32[4,2,32,16,128]{2,1,0,4,3:T(2,128)} %bitcast.543) | data formatting | bytes 4194304 | tf_op jit(solution)/shard_map/all_to_all | solution.py:165
  454.0 12.0 %copy.342 = f32[4,2,32,16,128]{4,2,3,0,1:T(8,128)} copy(f32[4,2,32,16,128]{2,1,0,4,3:T(2,128)} %bitcast.544) | data formatting | bytes 4194304 | tf_op jit(solution)/shard_map/all_to_all | solution.py:165
  (214 shorter events, 252.6 us)
Async XLA Ops:
  26.0 39.5 %all-to-all-start.4 = ((f32[8,1,8192]{2,1,0:T(1,128)}), f32[8,1,8192]{2,1,0:T(1,128)}, u32[]{:S(2)}, u32[]{:S(2)}) async-start(f32[8,1,8192]{2,1,0:T(1,128)} %reshape.1374), calls=%async_computation.4 | async-start | bytes 524288 | tf_op jit(solution)/shard_map/all_to_all | solution.py:146
  65.5 44.8 %all-to-all-start = ((f32[4,2,512,128]{3,0,1,2:T(4,128)}), f32[4,2,512,128]{3,0,1,2:T(4,128)S(1)}, u32[]{:S(2)}, u32[]{:S(2)}) async-start(f32[4,2,512,128]{3,0,1,2:T(4,128)} %copy.262), calls=%async_computation | async-start | bytes 4194304 | tf_op jit(solution)/shard_map/all_to_all | solution.py:104
  80.2 11.6 %collective-permute-start.1 = (f32[32,2048]{1,0:T(8,128)}, f32[32,2048]{1,0:T(8,128)}, u32[]{:S(2)}, u32[]{:S(2)}) collective-permute-start(f32[32,2048]{1,0:T(8,128)} %multiply_subtract_fusion.10), channel_id=1, source_target_pairs={{16,0},{32,16},{48,32},{64,48},{80,64},{96,80},{112,96},{17,1},{33... | collective-permute-start | bytes 786440 | tf_op jit(solution)/shard_map/ppermute | solution.py:12
  82.4 96.8 %collective-permute-start.2 = (f32[32,2048]{1,0:T(8,128)}, f32[32,2048]{1,0:T(8,128)}, u32[]{:S(2)}, u32[]{:S(2)}) collective-permute-start(f32[32,2048]{1,0:T(8,128)} %get-tuple-element.35), channel_id=1, source_target_pairs={{16,0},{32,16},{48,32},{64,48},{80,64},{96,80},{112,96},{17,1},{33... | collective-permute-start | bytes 786440 | tf_op jit(solution)/shard_map/ppermute | solution.py:12
  110.3 86.4 %all-to-all-start.2 = ((f32[8,1,8192]{2,1,0:T(1,128)}), f32[8,1,8192]{2,1,0:T(1,128)}, u32[]{:S(2)}, u32[]{:S(2)}) async-start(f32[8,1,8192]{2,1,0:T(1,128)} %reshape.1370), calls=%async_computation.2 | async-start | bytes 524288 | tf_op jit(solution)/shard_map/all_to_all | solution.py:147
  132.3 8.9 %copy-start.6 = (f32[4,32,64,32]{3,2,1,0:T(8,128)S(1)}, f32[4,32,64,32]{3,2,1,0:T(8,128)}, u32[]{:S(2)}) copy-start(f32[4,32,64,32]{3,2,1,0:T(8,128)} %reshape_squeeze.12) | copy-start | bytes 3145732
  132.3 8.9 %copy-start.9 = (f32[64,4,32,32]{0,3,2,1:T(8,128)S(1)}, f32[64,4,32,32]{0,3,2,1:T(8,128)}, u32[]{:S(2)}) copy-start(f32[64,4,32,32]{0,3,2,1:T(8,128)} %fusion.127) | copy-start | bytes 3145732
  141.2 6.8 %copy-start.4 = (f32[4,32,64,32]{3,2,1,0:T(8,128)S(1)}, f32[4,32,64,32]{3,2,1,0:T(8,128)}, u32[]{:S(2)}) copy-start(f32[4,32,64,32]{3,2,1,0:T(8,128)} %reshape_squeeze.13) | copy-start | bytes 3145732
  177.2 48.3 %copy-start.11 = (f32[1,2,32,2048]{3,2,1,0:T(8,128)}, f32[1,2,32,2048]{3,2,1,0:T(8,128)S(1)}, u32[]{:S(2)}) copy-start(f32[1,2,32,2048]{3,2,1,0:T(8,128)S(1)} %get-tuple-element.38) | copy-start | bytes 1572868
  177.2 48.3 %collective-permute-start = (f32[2,32,2048]{2,1,0:T(8,128)}, f32[2,32,2048]{2,1,0:T(8,128)}, u32[]{:S(2)}, u32[]{:S(2)}) collective-permute-start(f32[2,32,2048]{2,1,0:T(8,128)} %get-tuple-element.37), channel_id=1, source_target_pairs={{16,0},{32,16},{48,32},{64,48},{80,64},{96,80},{112,96},{17,1},{33... | collective-permute-start | bytes 1572872 | tf_op jit(solution)/shard_map/ppermute | solution.py:12
  196.7 22.2 %all-to-all-start.3 = ((f32[8,1,8192]{2,1,0:T(1,128)}), f32[8,1,8192]{2,1,0:T(1,128)}, u32[]{:S(2)}, u32[]{:S(2)}) async-start(f32[8,1,8192]{2,1,0:T(1,128)} %reshape.1372), calls=%async_computation.3 | async-start | bytes 524288 | tf_op jit(solution)/shard_map/all_to_all | solution.py:148
  207.5 18.0 %copy-start.19 = (f32[32,2048]{1,0:T(8,128)S(1)}, f32[32,2048]{1,0:T(8,128)}, u32[]{:S(2)}) copy-start(f32[32,2048]{1,0:T(8,128)} %get-tuple-element.62) | copy-start | bytes 786436
  234.3 9.4 %copy-start.13 = (f32[2048,1,1,32]{3,2,1,0:T(1,128)S(1)}, f32[2048,1,1,32]{3,2,1,0:T(1,128)}, u32[]{:S(2)}) copy-start(f32[2048,1,1,32]{3,2,1,0:T(1,128)} %reshape.1375) | copy-start | bytes 786436
  238.7 27.6 %all-to-all-start.1 = ((f32[8,1,16384]{2,1,0:T(1,128)}), f32[8,1,16384]{2,1,0:T(1,128)}, u32[]{:S(2)}, u32[]{:S(2)}) async-start(f32[8,1,16384]{2,1,0:T(1,128)} %reshape.1368), calls=%async_computation.1 | async-start | bytes 1048576 | tf_op jit(solution)/shard_map/all_to_all | solution.py:149
  246.6 17.0 %copy-start.33 = (f32[32,256]{0,1:T(8,128)S(1)}, f32[32,256]{0,1:T(8,128)}, u32[]{:S(2)}) copy-start(f32[32,256]{0,1:T(8,128)} %get-tuple-element.22) | copy-start | bytes 98308
  246.6 17.6 %copy-start.32 = (f32[32,256]{0,1:T(8,128)S(1)}, f32[32,256]{0,1:T(8,128)}, u32[]{:S(2)}) copy-start(f32[32,256]{0,1:T(8,128)} %get-tuple-element.21) | copy-start | bytes 98308
  246.6 18.3 %copy-start.31 = (f32[32,256]{0,1:T(8,128)S(1)}, f32[32,256]{0,1:T(8,128)}, u32[]{:S(2)}) copy-start(f32[32,256]{0,1:T(8,128)} %get-tuple-element.20) | copy-start | bytes 98308
  246.7 19.0 %copy-start.30 = (f32[32,256]{0,1:T(8,128)S(1)}, f32[32,256]{0,1:T(8,128)}, u32[]{:S(2)}) copy-start(f32[32,256]{0,1:T(8,128)} %get-tuple-element.19) | copy-start | bytes 98308
  278.4 19.9 %all-to-all-start.5 = ((f32[8,2,2,32,256]{4,3,2,1,0:T(8,128)}), f32[8,2,2,32,256]{4,3,2,1,0:T(8,128)S(1)}, u32[]{:S(2)}, u32[]{:S(2)}) async-start(f32[8,2,2,32,256]{4,3,2,1,0:T(8,128)} %pad_maximum_fusion.2), calls=%async_computation.5 | async-start | bytes 2097152 | tf_op jit(solution)/shard_map/all_to_all | solution.py:154
  320.5 9.1 %copy-start.7 = (f32[4,32,64,32]{3,2,1,0:T(8,128)S(1)}, f32[4,32,64,32]{3,2,1,0:T(8,128)}, u32[]{:S(2)}) copy-start(f32[4,32,64,32]{3,2,1,0:T(8,128)} %reshape_squeeze.14) | copy-start | bytes 3145732
  320.5 9.1 %copy-start.10 = (f32[64,4,32,32]{0,3,2,1:T(8,128)S(1)}, f32[64,4,32,32]{0,3,2,1:T(8,128)}, u32[]{:S(2)}) copy-start(f32[64,4,32,32]{0,3,2,1:T(8,128)} %fusion.123) | copy-start | bytes 3145732
  329.6 6.8 %copy-start.5 = (f32[4,32,64,32]{3,2,1,0:T(8,128)S(1)}, f32[4,32,64,32]{3,2,1,0:T(8,128)}, u32[]{:S(2)}) copy-start(f32[4,32,64,32]{3,2,1,0:T(8,128)} %reshape_squeeze.15) | copy-start | bytes 3145732
  343.3 5.3 %copy-start.3 = (f32[64,4,32,32]{0,3,2,1:T(8,128)}, f32[64,4,32,32]{0,3,2,1:T(8,128)S(1)}, u32[]{:S(2)}) copy-start(f32[64,4,32,32]{0,3,2,1:T(8,128)S(1)} %convolution_subtract_fusion) | copy-start | bytes 3145732
  390.5 36.8 %all-to-all-start.6 = ((f32[16,1,32768]{2,1,0:T(1,128)}), f32[16,1,32768]{2,1,0:T(1,128)}, u32[]{:S(2)}, u32[]{:S(2)}) async-start(f32[16,1,32768]{2,1,0:T(1,128)} %reshape.1376), calls=%async_computation.6 | async-start | bytes 4194304 | tf_op jit(solution)/shard_map/all_to_all | solution.py:165
  (23 other events, 53.3 us)
where the time goes:
time: 500 us; the launch traced here: 490 us
  local copies, waits for them, and re-layouts  152 us (30%)
  matrix products  139 us (28%)
  other arithmetic  103 us (21%)
  starting transfers between devices  47.9 us (10%)
  waiting for transfers between devices  44.9 us (9%)
    unnamed x92, local copies, waits for them, and re-layouts  51.9 us
    unnamed x6, other arithmetic  43.7 us
    all_to_all x1, waiting for transfers between devices, on_device(): lax.all_to_all(back_spectrum, 'pen', split_axis=3, concat_axis=2, tiled=T...  29.9 us
    dot_general x4, matrix products, factored_dft(): jnp.einsum('...uv,uw->...wv', real_grid, inner_cos, precision=HIGHEST)  24.7 us
    dot_general x4, matrix products, factored_dft(): jnp.einsum('...uv,uw->...wv', imag_grid, inner_cos, precision=HIGHEST)  24.2 us
    dot_general x4, matrix products, factored_dft(): jnp.einsum('...uv,uw->...wv', real_grid, inner_sin, precision=HIGHEST)  22.3 us
    all_to_all x2, local copies, waits for them, and re-layouts, on_device(): lax.all_to_all(back_spectrum, 'pen', split_axis=3, concat_axis=2, tiled=T...  22.2 us
    dot_general x4, matrix products, factored_dft(): jnp.einsum('...uv,uw->...wv', imag_grid, inner_sin, precision=HIGHEST)  19.1 us
  transfers between devices with their start and end apart: 10, of which 2 were waited for; matrix products, arithmetic and copies ran while one was open for 39% of the time, Pallas kernels for 0%

commit v1 on v0

v1 whole, which is shorter than its diff:
```python
import functools

import jax
import jax.numpy as jnp
import numpy as np
from jax import lax
from jax.experimental import pallas as pl
from jax.experimental.pallas import tpu as pltpu
from jax.sharding import Mesh, PartitionSpec as P

NX, NZ, KX, NY = 1024, 2048, 512, 32
HALF = NX // 2
PENS, WALLS = 16, 8
DEVICES = PENS * WALLS
OWN = KX // DEVICES
LOCAL = NY // WALLS
SLAB = NZ // PENS
ROWS = 2 * OWN
MIB = 1 << 20
F32, BF16 = jnp.float32, jnp.bfloat16

ORDER = ("core", "x", "y", "z")
SIZES = {"x": 4, "core": 2, "z": 4, "y": 4}


def strides():
    step, out = 1, {}
    for name in reversed(ORDER):
        out[name] = step
        step *= SIZES[name]
    return out


def wall_base(wall):
    s = strides()
    return (wall // 2) * s["x"] + (wall % 2) * s["core"]


def pen_offset(pen):
    s = strides()
    return (pen // 4) * s["z"] + (pen % 4) * s["y"]


def halves(table):
    high = np.asarray(table, np.float32).astype(jnp.bfloat16)
    low = (np.asarray(table, np.float64) - high.astype(np.float64)).astype(np.float32)
    return high, low.astype(jnp.bfloat16)


def stream_tables():
    point = np.arange(HALF)
    forward, backward = [], []
    for odd in (0, 1):
        mode = 2 * np.arange(KX // 2) + odd
        angle = 2.0 * np.pi * (mode[:, None] * point[None, :] % NX) / NX
        pair = np.stack([np.cos(angle), -np.sin(angle)], 1)
        pair = pair.reshape(-1, OWN, 2, HALF).transpose(0, 2, 1, 3).reshape(KX, HALF)
        weight = np.where(mode == 0, 1.0, 2.0) / (NX * NZ)
        weight = np.stack([weight, weight], 1).reshape(-1, OWN, 2).transpose(0, 2, 1)
        forward += halves(pair)
        backward += halves(pair * weight.reshape(KX, 1))
    return forward, backward


def span_tables():
    r = np.arange(SLAB)
    angle = 2.0 * np.pi * (r[:, None] * r[None, :] % SLAB) / SLAB
    high, low = halves(np.concatenate([np.cos(angle), np.sin(angle)], 1))
    turn = 2.0 * np.pi * (np.arange(PENS)[:, None] * r[None, :]) / NZ
    sign = np.where(np.arange(ROWS) < OWN, 1.0, -1.0)[None, :, None]
    cos = np.cos(turn)[:, None, :] * np.ones_like(sign)
    sin = np.sin(turn)[:, None, :] * sign
    return (
        np.concatenate([high, high], 0),
        low,
        cos.astype(np.float32),
        sin.astype(np.float32),
    )


def split(value):
    high = value.astype(BF16)
    return high, (value - high.astype(F32)).astype(BF16)


def sign_rows():
    row = lax.broadcasted_iota(jnp.int32, (ROWS, 128), 0)
    return jnp.where(row < OWN, 1.0, -1.0).astype(F32)


def swap(value):
    return pltpu.roll(value, OWN, axis=value.ndim - 2)


def stream_forward(x_ref, eh, el, oh, ol, out_ref):
    planes = x_ref.shape[0]
    x = x_ref[...].reshape(planes * SLAB, NX)
    first, second = x[:, :HALF], x[:, HALF:]
    dot = functools.partial(
        lax.dot_general, dimension_numbers=(((1,), (1,)), ((), ())), preferred_element_type=F32
    )
    owners = DEVICES // 2
    for value, high_ref, low_ref, base in (
        (first + second, eh, el, 0),
        (first - second, oh, ol, owners),
    ):
        high, low = split(value)
        table = high_ref[...]
        got = dot(table, high) + dot(table, low) + dot(low_ref[...], high)
        for j in range(planes):
            out_ref[base : base + owners, j] = got[:, j * SLAB : (j + 1) * SLAB].reshape(
                owners, ROWS, SLAB
            )


def stream_backward(y_ref, eh, el, oh, ol, out_ref):
    planes = out_ref.shape[0]
    owners = DEVICES // 2
    dot = functools.partial(jnp.dot, preferred_element_type=F32)
    sums = []
    for high_ref, low_ref, base in ((eh, el, 0), (oh, ol, owners)):
        value = jnp.concatenate(
            [y_ref[base : base + owners, j].reshape(KX, SLAB).T for j in range(planes)], 0
        )
        high, low = split(value)
        table = high_ref[...]
        sums.append(dot(high, table) + dot(low, table) + dot(high, low_ref[...]))
    even, odd = sums
    out_ref[:, :, :HALF] = (even + odd).reshape(planes, SLAB, HALF)
    out_ref[:, :, HALF:] = (even - odd).reshape(planes, SLAB, HALF)


def modified(index, length):
    return (2.0 * jnp.sin(np.float32(np.pi) * index.astype(F32) / length)) ** 2


def divisors(place_ref, table_ref, level_ref, stream_ref, span_ref, inverse_ref):
    place = place_ref[0]
    owners = DEVICES // 2
    odd = place // owners
    start = 2 * OWN * (place % owners) + odd
    row = lax.broadcasted_iota(jnp.int32, (ROWS, 128), 0) % OWN
    wave = jnp.zeros((ROWS, 128), jnp.int32)
    for i in range(OWN):
        wave = jnp.where(row == i, stream_ref[start + 2 * i], wave)
    wave_x = modified(wave, NX)
    wave_z = modified(span_ref[...], NZ)
    squared = wave_x[None] + wave_z[:, None, :]

    def step(j, ratio):
        level = level_ref[j]
        lower, upper, extra = (table_ref[level, k] for k in range(3))
        divisor = -(lower + upper + extra) - squared - lower * ratio
        inverse = 1.0 / divisor
        inverse_ref[j] = inverse
        return upper * inverse

    lax.fori_loop(0, NY, step, jnp.zeros((PENS, ROWS, 128), F32))


def fourier4(v, sign, forward):
    s02, d02, s13, d13 = v[0] + v[2], v[0] - v[2], v[1] + v[3], v[1] - v[3]
    turned = swap(d13) * sign
    up, down = d02 + turned, d02 - turned
    if not forward:
        up, down = down, up
    return [s02 + s13, up, s02 - s13, down]


def fourier16(v, sign, forward):
    inner = [fourier4([v[4 * a + b] for a in range(4)], sign, forward) for b in range(4)]
    out = [None] * 16
    for c in range(4):
        column = []
        for b in range(4):
            value = inner[b][c]
            if b * c == 4:
                value = swap(value) * (sign if forward else -sign)
            elif b * c:
                angle = 2.0 * np.pi * b * c / 16
                cos = np.float32(np.cos(angle))
                sin = np.float32(np.sin(angle) if forward else -np.sin(angle))
                value = value * cos + swap(value) * (sign * sin)
            column.append(value)
        for d, value in enumerate(fourier4(column, sign, forward)):
            out[c + 4 * d] = value
    return out


def span_dot(value, wide, narrow):
    high, low = split(value)
    return jnp.dot(
        jnp.concatenate([high, low], 1), wide, preferred_element_type=F32
    ) + jnp.dot(high, narrow, preferred_element_type=F32)


def span_solve(
    table_ref, level_ref, in_ref, inverse_ref, wide_ref, narrow_ref, cos_ref, sin_ref,
    out_ref, held_ref,
):
    sign = sign_rows()
    wide, narrow = wide_ref[...], narrow_ref[...]

    def forward(w, before):
        base = wall_base(w)
        turned = []
        for j in range(LOCAL):
            v = fourier16([in_ref[base + pen_offset(p), j] for p in range(PENS)], sign, True)
            for n in range(PENS):
                turned.append(v[n] * cos_ref[n] + swap(v[n]) * sin_ref[n] if n else v[0])
        got = span_dot(jnp.concatenate(turned, 0), wide, narrow)
        got = got.reshape(LOCAL, PENS, ROWS, 256)
        for j in range(LOCAL):
            plane = w * LOCAL + j
            lower = table_ref[level_ref[plane], 0]
            source = got[j, :, :, :128] + swap(got[j, :, :, 128:]) * sign
            before = (source - lower * before) * inverse_ref[plane]
            held_ref[plane] = before
        return before

    zero = jnp.zeros((PENS, ROWS, 128), F32)
    lax.fori_loop(0, WALLS, forward, zero)

    def backward(k, after):
        w = WALLS - 1 - k
        base = wall_base(w)
        solved = [None] * LOCAL
        for j in reversed(range(LOCAL)):
            plane = w * LOCAL + j
            upper = table_ref[level_ref[plane], 1]
            after = held_ref[plane] - upper * inverse_ref[plane] * after
            solved[j] = after.reshape(PENS * ROWS, 128)
        got = span_dot(jnp.concatenate(solved, 0), wide, narrow)
        got = got.reshape(LOCAL, PENS, ROWS, 256)
        for j in range(LOCAL):
            v = []
            for n in range(PENS):
                value = got[j, n, :, :128] - swap(got[j, n, :, 128:]) * sign
                v.append(value * cos_ref[n] - swap(value) * sin_ref[n] if n else value)
            for p, value in enumerate(fourier16(v, sign, False)):
                out_ref[base + pen_offset(p), j] = value
        return after

    lax.fori_loop(0, WALLS, backward, zero)


def params(mib):
    return pltpu.CompilerParams(vmem_limit_bytes=mib * MIB)


VMEM = pl.BlockSpec(memory_space=pltpu.VMEM)
SMEM = pl.BlockSpec(memory_space=pltpu.SMEM)
STEP = 2


def on_device(right_side, coef_table, stretch_index, stream_wave, span_wave):
    forward, backward = stream_tables()
    chunks = jax.ShapeDtypeStruct((DEVICES, LOCAL, ROWS, SLAB), F32)
    fixed = pl.BlockSpec((KX, HALF), lambda i: (0, 0))
    chunk_spec = pl.BlockSpec((DEVICES, STEP, ROWS, SLAB), lambda i: (0, i, 0, 0))
    field_spec = pl.BlockSpec((STEP, SLAB, NX), lambda i: (i, 0, 0))
    spectra = pl.pallas_call(
        stream_forward,
        grid=(LOCAL // STEP,),
        in_specs=[field_spec] + [fixed] * 4,
        out_specs=chunk_spec,
        out_shape=chunks,
        compiler_params=params(40),
        name="stream_forward",
    )(right_side, *forward)
    place = sum(lax.axis_index(n) * s for n, s in strides().items()).reshape(1)
    inverse = pl.pallas_call(
        divisors,
        in_specs=[SMEM] * 4 + [VMEM],
        out_specs=VMEM,
        out_shape=jax.ShapeDtypeStruct((NY, PENS, ROWS, 128), F32),
        compiler_params=params(40),
        cost_estimate=pl.CostEstimate(flops=10**7, bytes_accessed=2 * MIB, transcendentals=0),
        name="divisors",
    )(place, coef_table, stretch_index, stream_wave, span_wave.reshape(SLAB, PENS).T)
    spectra = lax.all_to_all(spectra, ORDER, 0, 0, tiled=True)
    wide, narrow, cos, sin = span_tables()
    solved = pl.pallas_call(
        span_solve,
        in_specs=[SMEM] * 2 + [VMEM] * 6,
        out_specs=VMEM,
        out_shape=chunks,
        scratch_shapes=[pltpu.VMEM((NY, PENS, ROWS, 128), F32)],
        compiler_params=params(40),
        name="span_solve",
    )(coef_table, stretch_index, spectra, inverse, wide, narrow, cos, sin)
    solved = lax.all_to_all(solved, ORDER, 0, 0, tiled=True)
    return pl.pallas_call(
        stream_backward,
        grid=(LOCAL // STEP,),
        in_specs=[chunk_spec] + [fixed] * 4,
        out_specs=field_spec,
        out_shape=jax.ShapeDtypeStruct(right_side.shape, F32),
        compiler_params=params(40),
        name="stream_backward",
    )(solved, *backward)


def solution(mesh):
    fine = Mesh(mesh.devices.reshape(4, 2, 4, 4), ("x", "core", "z", "y"))
    field = P(("x", "core"), ("z", "y"), None)
    return jax.shard_map(
        on_device,
        mesh=fine,
        in_specs=(field, P(), P(), P(), P()),
        out_specs=field,
        check_vma=False,
    )
```

time: 500 us -> 96.2 us (0.19); the launches traced: 490 us -> 95.4 us
  local copies, waits for them, and re-layouts: 152 us -> 8.96 us
  matrix products: 139 us -> 0 us
  other arithmetic: 103 us -> 0 us
  starting transfers between devices: 47.9 us -> 11.5 us
  blocking collectives: 0 us -> 34.9 us
  waiting for transfers between devices: 44.9 us -> 24.9 us
  Pallas kernels: 0 us -> 14.9 us
    dot_general x31 -> x0, matrix products: 139 us -> none  [the longest x4 24.7 us: factored_dft(): jnp.einsum('...uv,uw->...wv', real_grid, inner_cos, precision=HIGHEST)]
    unnamed x6 -> x0, other arithmetic: 43.7 us -> none
    unnamed x92 -> x39, local copies, waits for them, and re-layouts: 51.9 us -> 8.84 us
    all_to_all x0 -> x1, blocking collectives: none -> 34.9 us  [on_device(): solved = lax.all_to_all(solved, ORDER, 0, 0, tiled=True)]
    all_to_all x7 -> x1, starting transfers between devices: 41.7 us -> 11.5 us  [on_device(): spectra = lax.all_to_all(spectra, ORDER, 0, 0, tiled=True)]
    all_to_all x6 -> x0, local copies, waits for them, and re-layouts: 27 us -> none  [the longest x2 22.2 us: on_device(): lax.all_to_all(back_spectrum, 'pen', split_axis=3, concat_axis=2, tiled=T...]
    another operation x10 -> x0, local copies, waits for them, and re-layouts: 25.1 us -> none  [the longest x2 9.64 us: on_device(): back_spectrum = jnp.stack([out_real, out_imag], axis=1)]
    all_to_all x7 -> x1, waiting for transfers between devices: 44.9 us -> 24.9 us  [on_device(): spectra = lax.all_to_all(spectra, ORDER, 0, 0, tiled=True)]
  transfers between devices with their start and end apart: 10 -> 1, of which waited for: 2 -> 1; matrix products, arithmetic and copies ran while one was open for 39% -> 0% of each run, Pallas kernels for 0% -> 2%
where the time goes in v1:
time: 96.2 us; the launch traced here: 95.4 us
  blocking collectives  34.9 us (36%)
  waiting for transfers between devices  24.9 us (26%)
  Pallas kernels  14.9 us (15%)
  starting transfers between devices  11.5 us (12%)
  local copies, waits for them, and re-layouts  8.96 us (9%)
    all_to_all x1, blocking collectives, on_device(): solved = lax.all_to_all(solved, ORDER, 0, 0, tiled=True)  34.9 us
    all_to_all x1, waiting for transfers between devices, on_device(): spectra = lax.all_to_all(spectra, ORDER, 0, 0, tiled=True)  24.9 us
    all_to_all x1, starting transfers between devices, on_device(): spectra = lax.all_to_all(spectra, ORDER, 0, 0, tiled=True)  11.5 us
    unnamed x39, local copies, waits for them, and re-layouts  8.84 us
    pallas_call x1, Pallas kernels, on_device(): pl.pallas_call(span_solve, in_specs=[SMEM] * 2 + [VMEM] * 6, out_specs=VM...  6.59 us
    pallas_call x1, Pallas kernels, on_device(): pl.pallas_call(stream_backward, grid=(LOCAL // STEP,), in_specs=[chunk_sp...  3.26 us
    pallas_call x1, Pallas kernels, on_device(): pl.pallas_call(stream_forward, grid=(LOCAL // STEP,), in_specs=[field_spe...  3.03 us
    pallas_call x1, Pallas kernels, on_device(): pl.pallas_call(divisors, in_specs=[SMEM] * 4 + [VMEM], out_specs=VMEM, ou...  2.05 us
  transfers between devices with their start and end apart: 1, of which 1 were waited for; matrix products, arithmetic and copies ran while one was open for 0% of the time, Pallas kernels for 2%

profile of v1, /device:TPU:1, one launch (start us, length us, event | category | flops | bytes accessed | tf_op | source)
XLA Modules:
  0.0 95.4 jit_solution(5135689707034297177)
XLA Ops:
  0.0 1.6 %copy-done.2 = f32[4,128,1024]{2,1,0:T(8,128)S(1)} copy-done((f32[4,128,1024]{2,1,0:T(8,128)S(1)}, f32[4,128,1024]{2,1,0:T(8,128)}, u32[]{:S(2)}) %copy-start.2) | copy-done | bytes 2097176
  1.6 1.0 %copy-done.7 = bf16[512,512]{1,0:T(8,128)(2,1)S(1)} copy-done((bf16[512,512]{1,0:T(8,128)(2,1)S(1)}, bf16[512,512]{1,0:T(8,128)(2,1)}, u32[]{:S(2)}) %copy-start.7) | copy-done | bytes 524312
  2.6 1.0 %copy-done.8 = bf16[512,512]{1,0:T(8,128)(2,1)S(1)} copy-done((bf16[512,512]{1,0:T(8,128)(2,1)S(1)}, bf16[512,512]{1,0:T(8,128)(2,1)}, u32[]{:S(2)}) %copy-start.8) | copy-done | bytes 524312
  3.7 1.0 %copy-done.9 = bf16[512,512]{1,0:T(8,128)(2,1)S(1)} copy-done((bf16[512,512]{1,0:T(8,128)(2,1)S(1)}, bf16[512,512]{1,0:T(8,128)(2,1)}, u32[]{:S(2)}) %copy-start.9) | copy-done | bytes 524312
  4.7 1.0 %copy-done.10 = bf16[512,512]{1,0:T(8,128)(2,1)S(1)} copy-done((bf16[512,512]{1,0:T(8,128)(2,1)S(1)}, bf16[512,512]{1,0:T(8,128)(2,1)}, u32[]{:S(2)}) %copy-start.10) | copy-done | bytes 524312
  5.8 3.0 %stream_forward.1 = f32[128,4,8,128]{3,2,1,0:T(8,128)} custom-call(f32[4,128,1024]{2,1,0:T(8,128)S(1)} %copy-done.2, bf16[512,512]{1,0:T(8,128)(2,1)S(1)} %copy-done.7, bf16[512,512]{1,0:T(8,128)(2,1)S(1)} %copy-done.8, bf16[512,512]{1,0:T(8,128)(2,1)S(1)} %copy-done.9, bf16[512,512]{1,0:T(8,128)(2,1)S(1)} %copy-done.10), custom_call_target="tpu_custom_call" | custom-call | tf_op jit(solution)/shard_map/stream_forward/pallas_call | solution.py:262
  8.8 11.5 %all-to-all-start = ((f32[128,4,8,128]{3,2,1,0:T(8,128)}), f32[128,4,8,128]{3,2,1,0:T(8,128)S(1)}, u32[]{:S(2)}, u32[]{:S(2)}) async-start(f32[128,4,8,128]{3,2,1,0:T(8,128)} %stream_forward.1), calls=%async_computation | async-start | bytes 4194304 | tf_op jit(solution)/shard_map/all_to_all | solution.py:281
  20.3 0.0 copy-start.11
  20.3 0.0 copy-start.12
  20.3 0.0 copy-start.13
  20.4 0.0 copy-start.14
  20.4 0.1 copy.22.table_ref
  20.5 0.1 reshape.7
  20.6 0.1 copy.20
  20.6 2.1 %divisors.1.inverse_ref = f32[32,16,8,128]{3,2,1,0:T(8,128)S(1)} custom-call(s32[1]{0:T(128)} %bitcast.place_ref, f32[64,3]{1,0:T(8,128)S(1)} %copy.22.table_ref, s32[32]{0:T(128)S(1)} %copy-done.16, s32[512]{0:T(512)S(1)} %copy-done.15, s32[16,128]{1,0:T(8,128)S(1)} %bitcast.2), custom_call_target="tpu_custom_call" | custom-call | flops 10000000 | bytes 2097152 | tf_op jit(solution)/shard_map/divisors/pallas_call | solution.py:272
  22.7 1.3 %copy-done = f32[32,16,8,128]{3,2,1,0:T(8,128)} copy-done((f32[32,16,8,128]{3,2,1,0:T(8,128)}, f32[32,16,8,128]{3,2,1,0:T(8,128)S(1)}, u32[]{:S(2)}) %copy-start) | copy-done | bytes 2097176
  24.0 24.9 %all-to-all-done.in_ref = f32[128,4,8,128]{3,2,1,0:T(8,128)S(1)} async-done(((f32[128,4,8,128]{3,2,1,0:T(8,128)}), f32[128,4,8,128]{3,2,1,0:T(8,128)S(1)}, u32[]{:S(2)}, u32[]{:S(2)}) %all-to-all-start) | async-done | bytes 2097184 | tf_op jit(solution)/shard_map/all_to_all | solution.py:281
  49.0 1.6 %copy-done.1 = f32[32,16,8,128]{3,2,1,0:T(8,128)S(1)} copy-done((f32[32,16,8,128]{3,2,1,0:T(8,128)S(1)}, f32[32,16,8,128]{3,2,1,0:T(8,128)}, u32[]{:S(2)}) %copy-start.1) | copy-done | bytes 2097176
  50.5 6.6 %span_solve.1 = f32[128,4,8,128]{3,2,1,0:T(8,128)S(1)} custom-call(f32[64,3]{1,0:T(8,128)S(1)} %copy.22.table_ref, s32[32]{0:T(128)S(1)} %copy-done.16, f32[128,4,8,128]{3,2,1,0:T(8,128)S(1)} %all-to-all-done.in_ref, f32[32,16,8,128]{3,2,1,0:T(8,128)S(1)} %copy-done.1, bf16[256,256]{1,0:T(8,128)(2,1)S(1)} %copy-done.11, bf16[128,256]{1,0:T(8,128)(2,1)S(1)} %copy-done.12, ...), custom_call_target="tpu_custom_call" | custom-call | tf_op jit(solution)/shard_map/span_solve/pallas_call | solution.py:283
  57.1 0.0 copy-start.3
  57.1 0.0 copy-start.4
  57.2 0.0 copy-start.6
  57.2 34.9 %all_to_all.10.y_ref = f32[128,4,8,128]{3,2,1,0:T(8,128)S(1)} all-to-all(f32[128,4,8,128]{3,2,1,0:T(8,128)S(1)} %span_solve.1), channel_id=1, replica_groups=mesh['x'=4,'core'=2,'z'=4,'y'=4] {'core','x','y','z'}, dimensions={0} | all-to-all | bytes 4194304 | tf_op jit(solution)/shard_map/all_to_all | solution.py:292
  92.1 3.3 %stream_backward.1 = f32[4,128,1024]{2,1,0:T(8,128)} custom-call(f32[128,4,8,128]{3,2,1,0:T(8,128)S(1)} %all_to_all.10.y_ref, bf16[512,512]{1,0:T(8,128)(2,1)S(1)} %copy-done.3, bf16[512,512]{1,0:T(8,128)(2,1)S(1)} %copy-done.4, bf16[512,512]{1,0:T(8,128)(2,1)S(1)} %copy-done.5, bf16[512,512]{1,0:T(8,128)(2,1)S(1)} %copy-done.6), custom_call_target="tpu_custom_call" | custom-call | tf_op jit(solution)/shard_map/stream_backward/pallas_call | solution.py:293
  (24 shorter events, 0.0 us)
Async XLA Ops:
  0.0 1.6 %copy-start.2 = (f32[4,128,1024]{2,1,0:T(8,128)S(1)}, f32[4,128,1024]{2,1,0:T(8,128)}, u32[]{:S(2)}) copy-start(f32[4,128,1024]{2,1,0:T(8,128)} %x_ref.1) | copy-start | bytes 6291460
  1.6 1.0 %copy-start.7 = (bf16[512,512]{1,0:T(8,128)(2,1)S(1)}, bf16[512,512]{1,0:T(8,128)(2,1)}, u32[]{:S(2)}) copy-start(bf16[512,512]{1,0:T(8,128)(2,1)} %constant.47.clone.eh) | copy-start | bytes 1572868
  2.6 1.0 %copy-start.8 = (bf16[512,512]{1,0:T(8,128)(2,1)S(1)}, bf16[512,512]{1,0:T(8,128)(2,1)}, u32[]{:S(2)}) copy-start(bf16[512,512]{1,0:T(8,128)(2,1)} %constant.48.clone.el) | copy-start | bytes 1572868
  3.7 1.0 %copy-start.9 = (bf16[512,512]{1,0:T(8,128)(2,1)S(1)}, bf16[512,512]{1,0:T(8,128)(2,1)}, u32[]{:S(2)}) copy-start(bf16[512,512]{1,0:T(8,128)(2,1)} %constant.49.clone.oh) | copy-start | bytes 1572868
  4.7 1.0 %copy-start.10 = (bf16[512,512]{1,0:T(8,128)(2,1)S(1)}, bf16[512,512]{1,0:T(8,128)(2,1)}, u32[]{:S(2)}) copy-start(bf16[512,512]{1,0:T(8,128)(2,1)} %constant.50.clone.ol) | copy-start | bytes 1572868
  8.8 11.6 %copy-start.18 = (f32[64,3]{0,1:T(4,128)S(1)}, f32[64,3]{0,1:T(4,128)}, u32[]{:S(2)}) copy-start(f32[64,3]{0,1:T(4,128)} %param.18) | copy-start | bytes 2308
  8.8 11.7 %copy-start.17 = (s32[2048]{0:T(1024)S(1)}, s32[2048]{0:T(1024)}, u32[]{:S(2)}) copy-start(s32[2048]{0:T(1024)} %param.21) | copy-start | bytes 24580
  8.8 11.8 %copy-start.15 = (s32[512]{0:T(512)S(1)}, s32[512]{0:T(512)}, u32[]{:S(2)}) copy-start(s32[512]{0:T(512)} %stream_ref.1) | copy-start | bytes 6148
  8.8 11.8 %copy-start.16 = (s32[32]{0:T(128)S(1)}, s32[32]{0:T(128)}, u32[]{:S(2)}) copy-start(s32[32]{0:T(128)} %level_ref.3) | copy-start | bytes 388
  8.8 40.1 %all-to-all-start = ((f32[128,4,8,128]{3,2,1,0:T(8,128)}), f32[128,4,8,128]{3,2,1,0:T(8,128)S(1)}, u32[]{:S(2)}, u32[]{:S(2)}) async-start(f32[128,4,8,128]{3,2,1,0:T(8,128)} %stream_forward.1), calls=%async_computation | async-start | bytes 4194304 | tf_op jit(solution)/shard_map/all_to_all | solution.py:281
  20.3 28.6 %copy-start.11 = (bf16[256,256]{1,0:T(8,128)(2,1)S(1)}, bf16[256,256]{1,0:T(8,128)(2,1)}, u32[]{:S(2)}) copy-start(bf16[256,256]{1,0:T(8,128)(2,1)} %constant.51.clone.wide_ref) | copy-start | bytes 393220
  20.3 28.6 %copy-start.12 = (bf16[128,256]{1,0:T(8,128)(2,1)S(1)}, bf16[128,256]{1,0:T(8,128)(2,1)}, u32[]{:S(2)}) copy-start(bf16[128,256]{1,0:T(8,128)(2,1)} %constant.52.clone.narrow_ref) | copy-start | bytes 196612
  20.3 28.6 %copy-start.13 = (f32[16,8,128]{2,1,0:T(8,128)S(1)}, f32[16,8,128]{2,1,0:T(8,128)}, u32[]{:S(2)}) copy-start(f32[16,8,128]{2,1,0:T(8,128)} %constant.53.clone.cos_ref) | copy-start | bytes 196612
  20.4 28.6 %copy-start.14 = (f32[16,8,128]{2,1,0:T(8,128)S(1)}, f32[16,8,128]{2,1,0:T(8,128)}, u32[]{:S(2)}) copy-start(f32[16,8,128]{2,1,0:T(8,128)} %constant.54.clone.sin_ref) | copy-start | bytes 196612
  22.7 1.3 %copy-start = (f32[32,16,8,128]{3,2,1,0:T(8,128)}, f32[32,16,8,128]{3,2,1,0:T(8,128)S(1)}, u32[]{:S(2)}) copy-start(f32[32,16,8,128]{3,2,1,0:T(8,128)S(1)} %divisors.1.inverse_ref) | copy-start | bytes 6291460
  48.9 1.6 %copy-start.1 = (f32[32,16,8,128]{3,2,1,0:T(8,128)S(1)}, f32[32,16,8,128]{3,2,1,0:T(8,128)}, u32[]{:S(2)}) copy-start(f32[32,16,8,128]{3,2,1,0:T(8,128)} %copy-done) | copy-start | bytes 6291460
  57.1 35.0 %copy-start.3 = (bf16[512,512]{1,0:T(8,128)(2,1)S(1)}, bf16[512,512]{1,0:T(8,128)(2,1)}, u32[]{:S(2)}) copy-start(bf16[512,512]{1,0:T(8,128)(2,1)} %constant.55.clone.eh) | copy-start | bytes 1572868
  57.1 35.0 %copy-start.4 = (bf16[512,512]{1,0:T(8,128)(2,1)S(1)}, bf16[512,512]{1,0:T(8,128)(2,1)}, u32[]{:S(2)}) copy-start(bf16[512,512]{1,0:T(8,128)(2,1)} %constant.56.clone.el) | copy-start | bytes 1572868
  57.2 35.0 %copy-start.5 = (bf16[512,512]{1,0:T(8,128)(2,1)S(1)}, bf16[512,512]{1,0:T(8,128)(2,1)}, u32[]{:S(2)}) copy-start(bf16[512,512]{1,0:T(8,128)(2,1)} %constant.57.clone.oh) | copy-start | bytes 1572868
  57.2 35.0 %copy-start.6 = (bf16[512,512]{1,0:T(8,128)(2,1)S(1)}, bf16[512,512]{1,0:T(8,128)(2,1)}, u32[]{:S(2)}) copy-start(bf16[512,512]{1,0:T(8,128)(2,1)} %constant.58.clone.ol) | copy-start | bytes 1572868

commit v2 on v1

--- a/solution.py
+++ b/solution.py
@@ -92,25 +92,51 @@
     return pltpu.roll(value, OWN, axis=value.ndim - 2)
 
 
-def stream_forward(x_ref, eh, el, oh, ol, out_ref):
-    planes = x_ref.shape[0]
-    x = x_ref[...].reshape(planes * SLAB, NX)
-    first, second = x[:, :HALF], x[:, HALF:]
+def stream_forward(x_hbm, *refs):
+    tables, out_hbm, x_ref, table_refs, out_ref, x_sem, table_sems, out_sem = (
+        refs[:4], *refs[4:]
+    )
+    owners = DEVICES // 2
+    pairs = LOCAL // 2
+    loads = [
+        pltpu.make_async_copy(x_hbm.at[2 * i : 2 * i + 2], x_ref.at[2 * i : 2 * i + 2], x_sem.at[i])
+        for i in range(pairs)
+    ]
+    table_loads = [
+        pltpu.make_async_copy(tables[i], table_refs.at[i], table_sems.at[i]) for i in range(4)
+    ]
+    loads[0].start()
+    for load in table_loads + loads[1:]:
+        load.start()
     dot = functools.partial(
         lax.dot_general, dimension_numbers=(((1,), (1,)), ((), ())), preferred_element_type=F32
     )
-    owners = DEVICES // 2
-    for value, high_ref, low_ref, base in (
-        (first + second, eh, el, 0),
-        (first - second, oh, ol, owners),
-    ):
-        high, low = split(value)
-        table = high_ref[...]
-        got = dot(table, high) + dot(table, low) + dot(low_ref[...], high)
-        for j in range(planes):
-            out_ref[base : base + owners, j] = got[:, j * SLAB : (j + 1) * SLAB].reshape(
-                owners, ROWS, SLAB
+    stores = []
+    for i in range(pairs):
+        loads[i].wait()
+        x = x_ref[2 * i : 2 * i + 2].reshape(2 * SLAB, NX)
+        first, second = x[:, :HALF], x[:, HALF:]
+        for odd, value in enumerate((first + second, first - second)):
+            if i == 0:
+                table_loads[2 * odd].wait()
+                table_loads[2 * odd + 1].wait()
+            high, low = split(value)
+            table = table_refs[2 * odd]
+            got = dot(table, high) + dot(table, low) + dot(table_refs[2 * odd + 1], high)
+            base = odd * owners
+            for j in range(2):
+                out_ref[base : base + owners, 2 * i + j] = got[
+                    :, j * SLAB : (j + 1) * SLAB
+                ].reshape(owners, ROWS, SLAB)
+            region = (slice(base, base + owners), slice(2 * i, 2 * i + 2))
+            stores.append(
+                pltpu.make_async_copy(
+                    out_ref.at[region], out_hbm.at[region], out_sem.at[2 * i + odd]
+                )
             )
+            stores[-1].start()
+    for store in stores:
+        store.wait()
 
 
 def stream_backward(y_ref, eh, el, oh, ol, out_ref):
@@ -134,7 +160,9 @@
     return (2.0 * jnp.sin(np.float32(np.pi) * index.astype(F32) / length)) ** 2
 
 
-def divisors(place_ref, table_ref, level_ref, stream_ref, span_ref, inverse_ref):
+def divisors(
+    place_ref, table_ref, level_ref, stream_ref, span_ref, out_hbm, inverse_ref, sem
+):
     place = place_ref[0]
     owners = DEVICES // 2
     odd = place // owners
@@ -156,6 +184,9 @@
         return upper * inverse
 
     lax.fori_loop(0, NY, step, jnp.zeros((PENS, ROWS, 128), F32))
+    store = pltpu.make_async_copy(inverse_ref, out_hbm, sem)
+    store.start()
+    store.wait()
 
 
 def fourier4(v, sign, forward):
@@ -195,9 +226,15 @@
 
 
 def span_solve(
-    table_ref, level_ref, in_ref, inverse_ref, wide_ref, narrow_ref, cos_ref, sin_ref,
-    out_ref, held_ref,
+    table_ref, level_ref, in_ref, inverse_hbm, wide_ref, narrow_ref, cos_ref, sin_ref,
+    out_ref, held_ref, inverse_ref, sems,
 ):
+    def load(w):
+        part = pl.ds(w * LOCAL, LOCAL)
+        return pltpu.make_async_copy(inverse_hbm.at[part], inverse_ref.at[part], sems.at[w])
+
+    for w in range(WALLS):
+        load(w).start()
     sign = sign_rows()
     wide, narrow = wide_ref[...], narrow_ref[...]
 
@@ -210,6 +247,7 @@
                 turned.append(v[n] * cos_ref[n] + swap(v[n]) * sin_ref[n] if n else v[0])
         got = span_dot(jnp.concatenate(turned, 0), wide, narrow)
         got = got.reshape(LOCAL, PENS, ROWS, 256)
+        load(w).wait()
         for j in range(LOCAL):
             plane = w * LOCAL + j
             lower = table_ref[level_ref[plane], 0]
@@ -250,6 +288,7 @@
 
 VMEM = pl.BlockSpec(memory_space=pltpu.VMEM)
 SMEM = pl.BlockSpec(memory_space=pltpu.SMEM)
+HBM = pl.BlockSpec(memory_space=pltpu.HBM)
 STEP = 2
 
 
@@ -261,19 +300,27 @@
     field_spec = pl.BlockSpec((STEP, SLAB, NX), lambda i: (i, 0, 0))
     spectra = pl.pallas_call(
         stream_forward,
-        grid=(LOCAL // STEP,),
-        in_specs=[field_spec] + [fixed] * 4,
-        out_specs=chunk_spec,
+        in_specs=[HBM] * 5,
+        out_specs=HBM,
         out_shape=chunks,
-        compiler_params=params(40),
+        scratch_shapes=[
+            pltpu.VMEM((LOCAL, SLAB, NX), F32),
+            pltpu.VMEM((4, KX, HALF), BF16),
+            pltpu.VMEM(chunks.shape, F32),
+            pltpu.SemaphoreType.DMA((LOCAL // 2,)),
+            pltpu.SemaphoreType.DMA((4,)),
+            pltpu.SemaphoreType.DMA((LOCAL,)),
+        ],
+        compiler_params=params(60),
         name="stream_forward",
     )(right_side, *forward)
     place = sum(lax.axis_index(n) * s for n, s in strides().items()).reshape(1)
     inverse = pl.pallas_call(
         divisors,
         in_specs=[SMEM] * 4 + [VMEM],
-        out_specs=VMEM,
+        out_specs=HBM,
         out_shape=jax.ShapeDtypeStruct((NY, PENS, ROWS, 128), F32),
+        scratch_shapes=[pltpu.VMEM((NY, PENS, ROWS, 128), F32), pltpu.SemaphoreType.DMA(())],
         compiler_params=params(40),
         cost_estimate=pl.CostEstimate(flops=10**7, bytes_accessed=2 * MIB, transcendentals=0),
         name="divisors",
@@ -282,10 +329,11 @@
     wide, narrow, cos, sin = span_tables()
     solved = pl.pallas_call(
         span_solve,
-        in_specs=[SMEM] * 2 + [VMEM] * 6,
+        in_specs=[SMEM] * 2 + [VMEM, HBM] + [VMEM] * 4,
         out_specs=VMEM,
         out_shape=chunks,
-        scratch_shapes=[pltpu.VMEM((NY, PENS, ROWS, 128), F32)],
+        scratch_shapes=[pltpu.VMEM((NY, PENS, ROWS, 128), F32)] * 2
+        + [pltpu.SemaphoreType.DMA((WALLS,))],
         compiler_params=params(40),
         name="span_solve",
     )(coef_table, stretch_index, spectra, inverse, wide, narrow, cos, sin)

time: 96.2 us -> 93.2 us (0.969)
  local copies, waits for them, and re-layouts: 8.96 us -> 3.21 us
  Pallas kernels: 14.9 us -> 18.1 us
    unnamed x39 -> x29, local copies, waits for them, and re-layouts: 8.84 us -> 3.09 us
    pallas_call x3, Pallas kernels: 11.7 us -> 14.9 us  [the longest x1 7.01 us: on_device(): pl.pallas_call(span_solve, in_specs=[SMEM] * 2 + [VMEM, HBM] + [VMEM] * 4...]
where the time goes in v2:
time: 93.2 us; the launch traced here: 92.7 us
  blocking collectives  34.9 us (37%)
  waiting for transfers between devices  24.7 us (27%)
  Pallas kernels  18.1 us (19%)
  starting transfers between devices  11.5 us (12%)
  local copies, waits for them, and re-layouts  3.21 us (3%)
    all_to_all x1, blocking collectives, on_device(): solved = lax.all_to_all(solved, ORDER, 0, 0, tiled=True)  34.9 us
    all_to_all x1, waiting for transfers between devices, on_device(): spectra = lax.all_to_all(spectra, ORDER, 0, 0, tiled=True)  24.7 us
    all_to_all x1, starting transfers between devices, on_device(): spectra = lax.all_to_all(spectra, ORDER, 0, 0, tiled=True)  11.5 us
    pallas_call x1, Pallas kernels, on_device(): pl.pallas_call(span_solve, in_specs=[SMEM] * 2 + [VMEM, HBM] + [VMEM] * 4...  7.01 us
    pallas_call x1, Pallas kernels, on_device(): pl.pallas_call(stream_forward, in_specs=[HBM] * 5, out_specs=HBM, out_sha...  5.69 us
    pallas_call x1, Pallas kernels, on_device(): pl.pallas_call(stream_backward, grid=(LOCAL // STEP,), in_specs=[chunk_sp...  3.21 us
    unnamed x29, local copies, waits for them, and re-layouts  3.09 us
    pallas_call x1, Pallas kernels, on_device(): pl.pallas_call(divisors, in_specs=[SMEM] * 4 + [VMEM], out_specs=HBM, out...  2.23 us
  transfers between devices with their start and end apart: 1, of which 1 were waited for; matrix products, arithmetic and copies ran while one was open for 0% of the time, Pallas kernels for 2%

profile of v2, /device:TPU:1, one launch (start us, length us, event | category | flops | bytes accessed | tf_op | source)
XLA Modules:
  0.0 92.7 jit_solution(16623825151228983589)
XLA Ops:
  0.0 5.7 %stream_forward.1 = f32[128,4,8,128]{3,2,1,0:T(8,128)} custom-call(f32[4,128,1024]{2,1,0:T(8,128)} %x_hbm.1, bf16[512,512]{1,0:T(8,128)(2,1)} %constant.47.clone.refs_0_, bf16[512,512]{1,0:T(8,128)(2,1)} %constant.48.clone.refs_1_, bf16[512,512]{1,0:T(8,128)(2,1)} %constant.49.clone.refs_2_, bf16[512,512]{1,0:T(8,128)(2,1)} %constant.50.clone.refs_3_), custom_call_target="tpu_custom_call" | custom-call | tf_op jit(solution)/shard_map/stream_forward/pallas_call | solution.py:301
  5.7 0.0 copy-start.13
  5.7 0.0 copy-start.12
  5.7 0.0 copy-start.10
  5.7 0.0 copy-start.11
  5.7 11.5 %all-to-all-start = ((f32[128,4,8,128]{3,2,1,0:T(8,128)}), f32[128,4,8,128]{3,2,1,0:T(8,128)S(1)}, u32[]{:S(2)}, u32[]{:S(2)}) async-start(f32[128,4,8,128]{3,2,1,0:T(8,128)} %stream_forward.1), calls=%async_computation | async-start | bytes 4194304 | tf_op jit(solution)/shard_map/all_to_all | solution.py:328
  17.2 0.0 copy-start.6
  17.3 0.0 copy-start.7
  17.3 0.0 copy-start.8
  17.3 0.0 copy-start.9
  17.3 0.1 copy.22.table_ref
  17.4 0.1 reshape.7
  17.5 0.1 copy.20
  17.6 2.2 %divisors.1.inverse_hbm = f32[32,16,8,128]{3,2,1,0:T(8,128)S(1)} custom-call(s32[1]{0:T(128)} %bitcast.place_ref, f32[64,3]{1,0:T(8,128)S(1)} %copy.22.table_ref, s32[32]{0:T(128)S(1)} %copy-done.11, s32[512]{0:T(512)S(1)} %copy-done.10, s32[16,128]{1,0:T(8,128)S(1)} %bitcast.2), custom_call_target="tpu_custom_call" | custom-call | flops 10000000 | bytes 2097152 | tf_op jit(solution)/shard_map/divisors/pallas_call | solution.py:318
  19.8 1.3 %copy-done = f32[32,16,8,128]{3,2,1,0:T(8,128)} copy-done((f32[32,16,8,128]{3,2,1,0:T(8,128)}, f32[32,16,8,128]{3,2,1,0:T(8,128)S(1)}, u32[]{:S(2)}) %copy-start) | copy-done | bytes 2097176
  21.1 24.7 %all-to-all-done.in_ref = f32[128,4,8,128]{3,2,1,0:T(8,128)S(1)} async-done(((f32[128,4,8,128]{3,2,1,0:T(8,128)}), f32[128,4,8,128]{3,2,1,0:T(8,128)S(1)}, u32[]{:S(2)}, u32[]{:S(2)}) %all-to-all-start) | async-done | bytes 2097184 | tf_op jit(solution)/shard_map/all_to_all | solution.py:328
  45.9 1.6 %copy-done.1 = f32[32,16,8,128]{3,2,1,0:T(8,128)S(1)} copy-done((f32[32,16,8,128]{3,2,1,0:T(8,128)S(1)}, f32[32,16,8,128]{3,2,1,0:T(8,128)}, u32[]{:S(2)}) %copy-start.1) | copy-done | bytes 2097176
  47.5 7.0 %span_solve.1 = f32[128,4,8,128]{3,2,1,0:T(8,128)S(1)} custom-call(f32[64,3]{1,0:T(8,128)S(1)} %copy.22.table_ref, s32[32]{0:T(128)S(1)} %copy-done.11, f32[128,4,8,128]{3,2,1,0:T(8,128)S(1)} %all-to-all-done.in_ref, f32[32,16,8,128]{3,2,1,0:T(8,128)S(1)} %copy-done.1, bf16[256,256]{1,0:T(8,128)(2,1)S(1)} %copy-done.6, bf16[128,256]{1,0:T(8,128)(2,1)S(1)} %copy-done.7, ...), custom_call_target="tpu_custom_call" | custom-call | tf_op jit(solution)/shard_map/span_solve/pallas_call | solution.py:330
  54.5 0.0 copy-start.2
  54.5 0.0 copy-start.3
  54.5 0.0 copy-start.4
  54.5 0.0 copy-start.5
  54.5 34.9 %all_to_all.10.y_ref = f32[128,4,8,128]{3,2,1,0:T(8,128)S(1)} all-to-all(f32[128,4,8,128]{3,2,1,0:T(8,128)S(1)} %span_solve.1), channel_id=1, replica_groups=mesh['x'=4,'core'=2,'z'=4,'y'=4] {'core','x','y','z'}, dimensions={0} | all-to-all | bytes 4194304 | tf_op jit(solution)/shard_map/all_to_all | solution.py:340
  89.5 3.2 %stream_backward.1 = f32[4,128,1024]{2,1,0:T(8,128)} custom-call(f32[128,4,8,128]{3,2,1,0:T(8,128)S(1)} %all_to_all.10.y_ref, bf16[512,512]{1,0:T(8,128)(2,1)S(1)} %copy-done.2, bf16[512,512]{1,0:T(8,128)(2,1)S(1)} %copy-done.3, bf16[512,512]{1,0:T(8,128)(2,1)S(1)} %copy-done.4, bf16[512,512]{1,0:T(8,128)(2,1)S(1)} %copy-done.5), custom_call_target="tpu_custom_call" | custom-call | tf_op jit(solution)/shard_map/stream_backward/pallas_call | solution.py:341
  (14 shorter events, 0.0 us)
Async XLA Ops:
  5.7 11.6 %copy-start.13 = (f32[64,3]{0,1:T(4,128)S(1)}, f32[64,3]{0,1:T(4,128)}, u32[]{:S(2)}) copy-start(f32[64,3]{0,1:T(4,128)} %param.18) | copy-start | bytes 2308
  5.7 11.7 %copy-start.12 = (s32[2048]{0:T(1024)S(1)}, s32[2048]{0:T(1024)}, u32[]{:S(2)}) copy-start(s32[2048]{0:T(1024)} %param.21) | copy-start | bytes 24580
  5.7 11.8 %copy-start.10 = (s32[512]{0:T(512)S(1)}, s32[512]{0:T(512)}, u32[]{:S(2)}) copy-start(s32[512]{0:T(512)} %stream_ref.1) | copy-start | bytes 6148
  5.7 11.8 %copy-start.11 = (s32[32]{0:T(128)S(1)}, s32[32]{0:T(128)}, u32[]{:S(2)}) copy-start(s32[32]{0:T(128)} %level_ref.3) | copy-start | bytes 388
  5.7 40.1 %all-to-all-start = ((f32[128,4,8,128]{3,2,1,0:T(8,128)}), f32[128,4,8,128]{3,2,1,0:T(8,128)S(1)}, u32[]{:S(2)}, u32[]{:S(2)}) async-start(f32[128,4,8,128]{3,2,1,0:T(8,128)} %stream_forward.1), calls=%async_computation | async-start | bytes 4194304 | tf_op jit(solution)/shard_map/all_to_all | solution.py:328
  17.2 28.6 %copy-start.6 = (bf16[256,256]{1,0:T(8,128)(2,1)S(1)}, bf16[256,256]{1,0:T(8,128)(2,1)}, u32[]{:S(2)}) copy-start(bf16[256,256]{1,0:T(8,128)(2,1)} %constant.51.clone.wide_ref) | copy-start | bytes 393220
  17.3 28.6 %copy-start.7 = (bf16[128,256]{1,0:T(8,128)(2,1)S(1)}, bf16[128,256]{1,0:T(8,128)(2,1)}, u32[]{:S(2)}) copy-start(bf16[128,256]{1,0:T(8,128)(2,1)} %constant.52.clone.narrow_ref) | copy-start | bytes 196612
  17.3 28.6 %copy-start.8 = (f32[16,8,128]{2,1,0:T(8,128)S(1)}, f32[16,8,128]{2,1,0:T(8,128)}, u32[]{:S(2)}) copy-start(f32[16,8,128]{2,1,0:T(8,128)} %constant.53.clone.cos_ref) | copy-start | bytes 196612
  17.3 28.6 %copy-start.9 = (f32[16,8,128]{2,1,0:T(8,128)S(1)}, f32[16,8,128]{2,1,0:T(8,128)}, u32[]{:S(2)}) copy-start(f32[16,8,128]{2,1,0:T(8,128)} %constant.54.clone.sin_ref) | copy-start | bytes 196612
  19.8 1.3 %copy-start = (f32[32,16,8,128]{3,2,1,0:T(8,128)}, f32[32,16,8,128]{3,2,1,0:T(8,128)S(1)}, u32[]{:S(2)}) copy-start(f32[32,16,8,128]{3,2,1,0:T(8,128)S(1)} %divisors.1.inverse_hbm) | copy-start | bytes 6291460
  45.9 1.6 %copy-start.1 = (f32[32,16,8,128]{3,2,1,0:T(8,128)S(1)}, f32[32,16,8,128]{3,2,1,0:T(8,128)}, u32[]{:S(2)}) copy-start(f32[32,16,8,128]{3,2,1,0:T(8,128)} %copy-done) | copy-start | bytes 6291460
  54.5 35.0 %copy-start.2 = (bf16[512,512]{1,0:T(8,128)(2,1)S(1)}, bf16[512,512]{1,0:T(8,128)(2,1)}, u32[]{:S(2)}) copy-start(bf16[512,512]{1,0:T(8,128)(2,1)} %constant.55.clone.eh) | copy-start | bytes 1572868
  54.5 35.0 %copy-start.3 = (bf16[512,512]{1,0:T(8,128)(2,1)S(1)}, bf16[512,512]{1,0:T(8,128)(2,1)}, u32[]{:S(2)}) copy-start(bf16[512,512]{1,0:T(8,128)(2,1)} %constant.56.clone.el) | copy-start | bytes 1572868
  54.5 35.0 %copy-start.4 = (bf16[512,512]{1,0:T(8,128)(2,1)S(1)}, bf16[512,512]{1,0:T(8,128)(2,1)}, u32[]{:S(2)}) copy-start(bf16[512,512]{1,0:T(8,128)(2,1)} %constant.57.clone.oh) | copy-start | bytes 1572868
  54.5 35.0 %copy-start.5 = (bf16[512,512]{1,0:T(8,128)(2,1)S(1)}, bf16[512,512]{1,0:T(8,128)(2,1)}, u32[]{:S(2)}) copy-start(bf16[512,512]{1,0:T(8,128)(2,1)} %constant.58.clone.ol) | copy-start | bytes 1572868

commit v3 on v2

--- a/solution.py
+++ b/solution.py
@@ -65,17 +65,12 @@
 def span_tables():
     r = np.arange(SLAB)
     angle = 2.0 * np.pi * (r[:, None] * r[None, :] % SLAB) / SLAB
-    high, low = halves(np.concatenate([np.cos(angle), np.sin(angle)], 1))
+    cos, sin = np.cos(angle), np.sin(angle)
+    forward = halves(np.block([[cos, -sin], [sin, cos]]))
+    backward = halves(np.block([[cos, sin], [-sin, cos]]))
     turn = 2.0 * np.pi * (np.arange(PENS)[:, None] * r[None, :]) / NZ
-    sign = np.where(np.arange(ROWS) < OWN, 1.0, -1.0)[None, :, None]
-    cos = np.cos(turn)[:, None, :] * np.ones_like(sign)
-    sin = np.sin(turn)[:, None, :] * sign
-    return (
-        np.concatenate([high, high], 0),
-        low,
-        cos.astype(np.float32),
-        sin.astype(np.float32),
-    )
+    turn = np.broadcast_to(turn[:, None, :], (PENS, ROWS, SLAB))
+    return forward + backward + (np.cos(turn).astype(np.float32), np.sin(turn).astype(np.float32))
 
 
 def split(value):
@@ -83,13 +78,14 @@
     return high, (value - high.astype(F32)).astype(BF16)
 
 
-def sign_rows():
-    row = lax.broadcasted_iota(jnp.int32, (ROWS, 128), 0)
-    return jnp.where(row < OWN, 1.0, -1.0).astype(F32)
-
-
 def swap(value):
     return pltpu.roll(value, OWN, axis=value.ndim - 2)
+
+
+def exchange_rows(first, second):
+    row = lax.broadcasted_iota(jnp.int32, first.shape, first.ndim - 2)
+    top = row < OWN
+    return jnp.where(top, first, swap(second)), jnp.where(top, swap(first), second)
 
 
 def stream_forward(x_hbm, *refs):
@@ -124,11 +120,12 @@
             table = table_refs[2 * odd]
             got = dot(table, high) + dot(table, low) + dot(table_refs[2 * odd + 1], high)
             base = odd * owners
-            for j in range(2):
-                out_ref[base : base + owners, 2 * i + j] = got[
-                    :, j * SLAB : (j + 1) * SLAB
-                ].reshape(owners, ROWS, SLAB)
-            region = (slice(base, base + owners), slice(2 * i, 2 * i + 2))
+            parts = exchange_rows(
+                *(got[:, j * SLAB : (j + 1) * SLAB].reshape(owners, ROWS, SLAB) for j in (0, 1))
+            )
+            for part in (0, 1):
+                out_ref[base : base + owners, i, part] = parts[part]
+            region = (slice(base, base + owners), i)
             stores.append(
                 pltpu.make_async_copy(
                     out_ref.at[region], out_hbm.at[region], out_sem.at[2 * i + odd]
@@ -140,20 +137,18 @@
 
 
 def stream_backward(y_ref, eh, el, oh, ol, out_ref):
-    planes = out_ref.shape[0]
     owners = DEVICES // 2
     dot = functools.partial(jnp.dot, preferred_element_type=F32)
     sums = []
     for high_ref, low_ref, base in ((eh, el, 0), (oh, ol, owners)):
-        value = jnp.concatenate(
-            [y_ref[base : base + owners, j].reshape(KX, SLAB).T for j in range(planes)], 0
-        )
+        planes = exchange_rows(*(y_ref[base : base + owners, 0, part] for part in (0, 1)))
+        value = jnp.concatenate([plane.reshape(KX, SLAB).T for plane in planes], 0)
         high, low = split(value)
         table = high_ref[...]
         sums.append(dot(high, table) + dot(low, table) + dot(high, low_ref[...]))
     even, odd = sums
-    out_ref[:, :, :HALF] = (even + odd).reshape(planes, SLAB, HALF)
-    out_ref[:, :, HALF:] = (even - odd).reshape(planes, SLAB, HALF)
+    out_ref[:, :, :HALF] = (even + odd).reshape(2, SLAB, HALF)
+    out_ref[:, :, HALF:] = (even - odd).reshape(2, SLAB, HALF)
 
 
 def modified(index, length):
@@ -189,97 +184,140 @@
     store.wait()
 
 
-def fourier4(v, sign, forward):
-    s02, d02, s13, d13 = v[0] + v[2], v[0] - v[2], v[1] + v[3], v[1] - v[3]
-    turned = swap(d13) * sign
-    up, down = d02 + turned, d02 - turned
-    if not forward:
-        up, down = down, up
-    return [s02 + s13, up, s02 - s13, down]
-
-
-def fourier16(v, sign, forward):
-    inner = [fourier4([v[4 * a + b] for a in range(4)], sign, forward) for b in range(4)]
+def fourier4(v, sign):
+    (r0, i0), (r1, i1), (r2, i2), (r3, i3) = v
+    sr, si, dr, di = r0 + r2, i0 + i2, r0 - r2, i0 - i2
+    tr, ti, er, ei = r1 + r3, i1 + i3, r1 - r3, i1 - i3
+    if sign < 0:
+        one, three = (dr + ei, di - er), (dr - ei, di + er)
+    else:
+        one, three = (dr - ei, di + er), (dr + ei, di - er)
+    return [(sr + tr, si + ti), one, (sr - tr, si - ti), three]
+
+
+def turned(v, steps, sign):
+    re, im = v
+    angle = 2.0 * np.pi * steps / 16
+    cos, sin = np.float32(np.cos(angle)), np.float32(sign * np.sin(angle))
+    if steps == 0:
+        return v
+    if steps == 4:
+        return (im, -re) if sign < 0 else (-im, re)
+    if steps == 2:
+        half = np.float32(np.sqrt(0.5))
+        if sign < 0:
+            return ((re + im) * half, (im - re) * half)
+        return ((re - im) * half, (im + re) * half)
+    return (re * cos - im * sin, im * cos + re * sin)
+
+
+def fourier16(v, sign):
+    inner = [fourier4([v[4 * a + b] for a in range(4)], sign) for b in range(4)]
     out = [None] * 16
     for c in range(4):
-        column = []
-        for b in range(4):
-            value = inner[b][c]
-            if b * c == 4:
-                value = swap(value) * (sign if forward else -sign)
-            elif b * c:
-                angle = 2.0 * np.pi * b * c / 16
-                cos = np.float32(np.cos(angle))
-                sin = np.float32(np.sin(angle) if forward else -np.sin(angle))
-                value = value * cos + swap(value) * (sign * sin)
-            column.append(value)
-        for d, value in enumerate(fourier4(column, sign, forward)):
+        column = [turned(inner[b][c], b * c, sign) for b in range(4)]
+        for d, value in enumerate(fourier4(column, sign)):
             out[c + 4 * d] = value
     return out
 
 
-def span_dot(value, wide, narrow):
-    high, low = split(value)
-    return jnp.dot(
-        jnp.concatenate([high, low], 1), wide, preferred_element_type=F32
-    ) + jnp.dot(high, narrow, preferred_element_type=F32)
+def span_dot(parts, high_table, low_table):
+    high, low = parts
+    dot = functools.partial(jnp.dot, preferred_element_type=F32)
+    return dot(high, high_table) + dot(low, high_table) + dot(high, low_table)
 
 
 def span_solve(
-    table_ref, level_ref, in_ref, inverse_hbm, wide_ref, narrow_ref, cos_ref, sin_ref,
+    table_ref, level_ref, in_ref, inverse_hbm, fh, fl, bh, bl, cos_ref, sin_ref,
     out_ref, held_ref, inverse_ref, sems,
 ):
-    def load(w):
-        part = pl.ds(w * LOCAL, LOCAL)
-        return pltpu.make_async_copy(inverse_hbm.at[part], inverse_ref.at[part], sems.at[w])
-
+    loads = []
     for w in range(WALLS):
-        load(w).start()
-    sign = sign_rows()
-    wide, narrow = wide_ref[...], narrow_ref[...]
-
-    def forward(w, before):
+        part = slice(w * LOCAL, (w + 1) * LOCAL)
+        loads.append(
+            pltpu.make_async_copy(inverse_hbm.at[part], inverse_ref.at[part], sems.at[w])
+        )
+        loads[-1].start()
+    pairs = LOCAL // 2
+
+    def gather(w):
         base = wall_base(w)
-        turned = []
-        for j in range(LOCAL):
-            v = fourier16([in_ref[base + pen_offset(p), j] for p in range(PENS)], sign, True)
-            for n in range(PENS):
-                turned.append(v[n] * cos_ref[n] + swap(v[n]) * sin_ref[n] if n else v[0])
-        got = span_dot(jnp.concatenate(turned, 0), wide, narrow)
-        got = got.reshape(LOCAL, PENS, ROWS, 256)
-        load(w).wait()
-        for j in range(LOCAL):
-            plane = w * LOCAL + j
-            lower = table_ref[level_ref[plane], 0]
-            source = got[j, :, :, :128] + swap(got[j, :, :, 128:]) * sign
-            before = (source - lower * before) * inverse_ref[plane]
-            held_ref[plane] = before
+        real, imag = [], []
+        for i in range(pairs):
+            v = [
+                tuple(in_ref[base + pen_offset(p), i, part] for part in (0, 1))
+                for p in range(PENS)
+            ]
+            for n, (re, im) in enumerate(fourier16(v, -1)):
+                if n:
+                    cos, sin = cos_ref[n], sin_ref[n]
+                    re, im = re * cos + im * sin, im * cos - re * sin
+                real.append(re)
+                imag.append(im)
+        return split(
+            jnp.concatenate([jnp.concatenate(real, 0), jnp.concatenate(imag, 0)], 1)
+        )
+
+    def eliminate(w, got, before):
+        got = got.reshape(pairs, PENS, ROWS, 2 * SLAB)
+        loads[w].wait()
+        for i in range(pairs):
+            planes = exchange_rows(got[i, :, :, :SLAB], got[i, :, :, SLAB:])
+            for j, source in enumerate(planes):
+                plane = w * LOCAL + 2 * i + j
+                if plane:
+                    source = source - table_ref[level_ref[plane], 0] * before
+                before = source * inverse_ref[plane]
+                held_ref[plane] = before
         return before
 
-    zero = jnp.zeros((PENS, ROWS, 128), F32)
-    lax.fori_loop(0, WALLS, forward, zero)
-
-    def backward(k, after):
-        w = WALLS - 1 - k
+    def substitute(w, after):
+        real, imag = [], []
+        for i in reversed(range(pairs)):
+            planes = [None, None]
+            for j in (1, 0):
+                plane = w * LOCAL + 2 * i + j
+                value = held_ref[plane]
+                if plane < NY - 1:
+                    upper = table_ref[level_ref[plane], 1]
+                    value = value - upper * inverse_ref[plane] * after
+                planes[j] = after = value
+            re, im = exchange_rows(*planes)
+            real.insert(0, re.reshape(PENS * ROWS, SLAB))
+            imag.insert(0, im.reshape(PENS * ROWS, SLAB))
+        return after, split(
+            jnp.concatenate([jnp.concatenate(real, 0), jnp.concatenate(imag, 0)], 1)
+        )
+
+    def scatter(w, got):
         base = wall_base(w)
-        solved = [None] * LOCAL
-        for j in reversed(range(LOCAL)):
-            plane = w * LOCAL + j
-            upper = table_ref[level_ref[plane], 1]
-            after = held_ref[plane] - upper * inverse_ref[plane] * after
-            solved[j] = after.reshape(PENS * ROWS, 128)
-        got = span_dot(jnp.concatenate(solved, 0), wide, narrow)
-        got = got.reshape(LOCAL, PENS, ROWS, 256)
-        for j in range(LOCAL):
+        got = got.reshape(pairs, PENS, ROWS, 2 * SLAB)
+        for i in range(pairs):
             v = []
             for n in range(PENS):
-                value = got[j, n, :, :128] - swap(got[j, n, :, 128:]) * sign
-                v.append(value * cos_ref[n] - swap(value) * sin_ref[n] if n else value)
-            for p, value in enumerate(fourier16(v, sign, False)):
-                out_ref[base + pen_offset(p), j] = value
-        return after
-
-    lax.fori_loop(0, WALLS, backward, zero)
+                re, im = got[i, n, :, :SLAB], got[i, n, :, SLAB:]
+                if n:
+                    cos, sin = cos_ref[n], sin_ref[n]
+                    re, im = re * cos - im * sin, im * cos + re * sin
+                v.append((re, im))
+            for p, value in enumerate(fourier16(v, 1)):
+                for part in (0, 1):
+                    out_ref[base + pen_offset(p), i, part] = value[part]
+
+    high, low = fh[...], fl[...]
+    parts, before = gather(0), None
+    for w in range(WALLS):
+        got = span_dot(parts, high, low)
+        if w + 1 < WALLS:
+            parts = gather(w + 1)
+        before = eliminate(w, got, before)
+    high, low = bh[...], bl[...]
+    after, parts = substitute(WALLS - 1, None)
+    for w in reversed(range(WALLS)):
+        got = span_dot(parts, high, low)
+        if w:
+            after, parts = substitute(w - 1, after)
+        scatter(w, got)
 
 
 def params(mib):
@@ -294,9 +332,9 @@
 
 def on_device(right_side, coef_table, stretch_index, stream_wave, span_wave):
     forward, backward = stream_tables()
-    chunks = jax.ShapeDtypeStruct((DEVICES, LOCAL, ROWS, SLAB), F32)
+    chunks = jax.ShapeDtypeStruct((DEVICES, LOCAL // 2, 2, ROWS, SLAB), F32)
     fixed = pl.BlockSpec((KX, HALF), lambda i: (0, 0))
-    chunk_spec = pl.BlockSpec((DEVICES, STEP, ROWS, SLAB), lambda i: (0, i, 0, 0))
+    chunk_spec = pl.BlockSpec((DEVICES, 1, 2, ROWS, SLAB), lambda i: (0, i, 0, 0, 0))
     field_spec = pl.BlockSpec((STEP, SLAB, NX), lambda i: (i, 0, 0))
     spectra = pl.pallas_call(
         stream_forward,
@@ -321,22 +359,21 @@
         out_specs=HBM,
         out_shape=jax.ShapeDtypeStruct((NY, PENS, ROWS, 128), F32),
         scratch_shapes=[pltpu.VMEM((NY, PENS, ROWS, 128), F32), pltpu.SemaphoreType.DMA(())],
-        compiler_params=params(40),
+        compiler_params=params(60),
         cost_estimate=pl.CostEstimate(flops=10**7, bytes_accessed=2 * MIB, transcendentals=0),
         name="divisors",
     )(place, coef_table, stretch_index, stream_wave, span_wave.reshape(SLAB, PENS).T)
     spectra = lax.all_to_all(spectra, ORDER, 0, 0, tiled=True)
-    wide, narrow, cos, sin = span_tables()
     solved = pl.pallas_call(
         span_solve,
-        in_specs=[SMEM] * 2 + [VMEM, HBM] + [VMEM] * 4,
+        in_specs=[SMEM] * 2 + [VMEM, HBM] + [VMEM] * 6,
         out_specs=VMEM,
         out_shape=chunks,
         scratch_shapes=[pltpu.VMEM((NY, PENS, ROWS, 128), F32)] * 2
         + [pltpu.SemaphoreType.DMA((WALLS,))],
-        compiler_params=params(40),
+        compiler_params=params(48),
         name="span_solve",
-    )(coef_table, stretch_index, spectra, inverse, wide, narrow, cos, sin)
+    )(coef_table, stretch_index, spectra, inverse, *span_tables())
     solved = lax.all_to_all(solved, ORDER, 0, 0, tiled=True)
     return pl.pallas_call(
         stream_backward,

time: 93.2 us -> 91.2 us (0.979)
  local copies, waits for them, and re-layouts: 3.21 us -> 1.53 us
  waiting for transfers between devices: 24.7 us -> 23.5 us
    unnamed x29, local copies, waits for them, and re-layouts: 3.09 us -> 0.79 us
    pallas_call x1, Pallas kernels: 2.23 us -> 3.51 us  [on_device(): pl.pallas_call(divisors, in_specs=[SMEM] * 4 + [VMEM], out_specs=HBM, out...]
    all_to_all x1, waiting for transfers between devices: 24.7 us -> 23.5 us  [on_device(): spectra = lax.all_to_all(spectra, ORDER, 0, 0, tiled=True)]
  transfers between devices with their start and end apart: 1 -> 1, of which waited for: 1 -> 1; matrix products, arithmetic and copies ran while one was open for 0% -> 2% of each run, Pallas kernels for 2% -> 4%
where the time goes in v3:
time: 91.2 us; the launch traced here: 90.6 us
  blocking collectives  34.9 us (38%)
  waiting for transfers between devices  23.5 us (26%)
  Pallas kernels  18.9 us (21%)
  starting transfers between devices  11.5 us (13%)
  local copies, waits for them, and re-layouts  1.53 us (2%)
    all_to_all x1, blocking collectives, on_device(): solved = lax.all_to_all(solved, ORDER, 0, 0, tiled=True)  34.9 us
    all_to_all x1, waiting for transfers between devices, on_device(): spectra = lax.all_to_all(spectra, ORDER, 0, 0, tiled=True)  23.5 us
    all_to_all x1, starting transfers between devices, on_device(): spectra = lax.all_to_all(spectra, ORDER, 0, 0, tiled=True)  11.5 us
    pallas_call x1, Pallas kernels, on_device(): pl.pallas_call(span_solve, in_specs=[SMEM] * 2 + [VMEM, HBM] + [VMEM] * 6...  6.45 us
    pallas_call x1, Pallas kernels, on_device(): pl.pallas_call(stream_forward, in_specs=[HBM] * 5, out_specs=HBM, out_sha...  5.69 us
    pallas_call x1, Pallas kernels, on_device(): pl.pallas_call(divisors, in_specs=[SMEM] * 4 + [VMEM], out_specs=HBM, out...  3.51 us
    pallas_call x1, Pallas kernels, on_device(): pl.pallas_call(stream_backward, grid=(LOCAL // STEP,), in_specs=[chunk_sp...  3.22 us
  transfers between devices with their start and end apart: 1, of which 1 were waited for; matrix products, arithmetic and copies ran while one was open for 2% of the time, Pallas kernels for 4%

profile of v3, /device:TPU:1, one launch (start us, length us, event | category | flops | bytes accessed | tf_op | source)
XLA Modules:
  0.0 90.6 jit_solution(6212383948574885804)
XLA Ops:
  0.0 5.7 %stream_forward.1 = f32[128,2,2,8,128]{4,3,2,1,0:T(8,128)} custom-call(f32[4,128,1024]{2,1,0:T(8,128)} %x_hbm.1, bf16[512,512]{1,0:T(8,128)(2,1)} %constant.51.clone.refs_0_, bf16[512,512]{1,0:T(8,128)(2,1)} %constant.52.clone.refs_1_, bf16[512,512]{1,0:T(8,128)(2,1)} %constant.53.clone.refs_2_, bf16[512,512]{1,0:T(8,128)(2,1)} %constant.54.clone.refs_3_), custom_call_target="tpu_custom_call" | custom-call | tf_op jit(solution)/shard_map/stream_forward/pallas_call | solution.py:339
  5.7 0.0 copy-start.13
  5.7 0.0 copy-start.12
  5.7 11.5 %all-to-all-start = ((f32[128,2,2,8,128]{4,3,2,1,0:T(8,128)}), f32[128,2,2,8,128]{4,3,2,1,0:T(8,128)S(1)}, u32[]{:S(2)}, u32[]{:S(2)}) async-start(f32[128,2,2,8,128]{4,3,2,1,0:T(8,128)} %stream_forward.1), calls=%async_computation | async-start | bytes 4194304 | tf_op jit(solution)/shard_map/all_to_all | solution.py:366
  17.2 0.0 copy-start.5
  17.2 0.0 copy-start.6
  17.2 0.0 copy-start.7
  17.3 0.0 copy-start.8
  17.3 0.0 copy-start.9
  17.3 0.0 copy-start.10
  17.3 0.0 copy-start.11
  17.3 0.7 copy.24.table_ref
  18.0 0.1 reshape.7
  18.1 0.7 copy.22
  18.8 3.5 %divisors.1.inverse_hbm = f32[32,16,8,128]{3,2,1,0:T(8,128)} custom-call(s32[1]{0:T(128)} %bitcast.place_ref, f32[64,3]{1,0:T(8,128)} %copy.24.table_ref, s32[32]{0:T(128)} %level_ref.3, s32[512]{0:T(512)} %stream_ref.1, s32[16,128]{1,0:T(8,128)} %bitcast.2), custom_call_target="tpu_custom_call" | custom-call | flops 10000000 | bytes 2097152 | tf_op jit(solution)/shard_map/divisors/pallas_call | solution.py:356
  22.3 23.5 %all-to-all-done.in_ref = f32[128,2,2,8,128]{4,3,2,1,0:T(8,128)S(1)} async-done(((f32[128,2,2,8,128]{4,3,2,1,0:T(8,128)}), f32[128,2,2,8,128]{4,3,2,1,0:T(8,128)S(1)}, u32[]{:S(2)}, u32[]{:S(2)}) %all-to-all-start) | async-done | bytes 2097184 | tf_op jit(solution)/shard_map/all_to_all | solution.py:366
  45.8 0.0 copy-done.7
  45.9 6.5 %span_solve.1 = f32[128,2,2,8,128]{4,3,2,1,0:T(8,128)S(1)} custom-call(f32[64,3]{1,0:T(8,128)S(1)} %copy-done.4, s32[32]{0:T(128)S(1)} %copy-done.11, f32[128,2,2,8,128]{4,3,2,1,0:T(8,128)S(1)} %all-to-all-done.in_ref, f32[32,16,8,128]{3,2,1,0:T(8,128)} %divisors.1.inverse_hbm, bf16[256,256]{1,0:T(8,128)(2,1)S(1)} %copy-done.5, ...), custom_call_target="tpu_custom_call" | custom-call | tf_op jit(solution)/shard_map/span_solve/pallas_call | solution.py:367
  52.4 0.0 copy-start
  52.4 0.0 copy-start.1
  52.4 0.0 copy-start.2
  52.4 0.0 copy-start.3
  52.4 34.9 %all_to_all.10.y_ref = f32[128,2,2,8,128]{4,3,2,1,0:T(8,128)S(1)} all-to-all(f32[128,2,2,8,128]{4,3,2,1,0:T(8,128)S(1)} %span_solve.1), channel_id=1, replica_groups=mesh['x'=4,'core'=2,'z'=4,'y'=4] {'core','x','y','z'}, dimensions={0} | all-to-all | bytes 4194304 | tf_op jit(solution)/shard_map/all_to_all | solution.py:377
  87.4 3.2 %stream_backward.1 = f32[4,128,1024]{2,1,0:T(8,128)} custom-call(f32[128,2,2,8,128]{4,3,2,1,0:T(8,128)S(1)} %all_to_all.10.y_ref, bf16[512,512]{1,0:T(8,128)(2,1)S(1)} %copy-done, bf16[512,512]{1,0:T(8,128)(2,1)S(1)} %copy-done.1, bf16[512,512]{1,0:T(8,128)(2,1)S(1)} %copy-done.2, bf16[512,512]{1,0:T(8,128)(2,1)S(1)} %copy-done.3), custom_call_target="tpu_custom_call" | custom-call | tf_op jit(solution)/shard_map/stream_backward/pallas_call | solution.py:378
  (14 shorter events, 0.0 us)
Async XLA Ops:
  5.7 11.6 %copy-start.13 = (f32[64,3]{0,1:T(4,128)S(1)}, f32[64,3]{0,1:T(4,128)}, u32[]{:S(2)}) copy-start(f32[64,3]{0,1:T(4,128)} %param.20) | copy-start | bytes 2308
  5.7 12.3 %copy-start.12 = (s32[2048]{0:T(1024)S(1)}, s32[2048]{0:T(1024)}, u32[]{:S(2)}) copy-start(s32[2048]{0:T(1024)} %param.23) | copy-start | bytes 24580
  5.7 40.1 %all-to-all-start = ((f32[128,2,2,8,128]{4,3,2,1,0:T(8,128)}), f32[128,2,2,8,128]{4,3,2,1,0:T(8,128)S(1)}, u32[]{:S(2)}, u32[]{:S(2)}) async-start(f32[128,2,2,8,128]{4,3,2,1,0:T(8,128)} %stream_forward.1), calls=%async_computation | async-start | bytes 4194304 | tf_op jit(solution)/shard_map/all_to_all | solution.py:366
  17.2 28.6 %copy-start.5 = (bf16[256,256]{1,0:T(8,128)(2,1)S(1)}, bf16[256,256]{1,0:T(8,128)(2,1)}, u32[]{:S(2)}) copy-start(bf16[256,256]{1,0:T(8,128)(2,1)} %constant.55.clone.fh) | copy-start | bytes 393220
  17.2 28.6 %copy-start.6 = (bf16[256,256]{1,0:T(8,128)(2,1)S(1)}, bf16[256,256]{1,0:T(8,128)(2,1)}, u32[]{:S(2)}) copy-start(bf16[256,256]{1,0:T(8,128)(2,1)} %constant.56.clone.fl) | copy-start | bytes 393220
  17.2 28.6 %copy-start.7 = (bf16[256,256]{1,0:T(8,128)(2,1)S(1)}, bf16[256,256]{1,0:T(8,128)(2,1)}, u32[]{:S(2)}) copy-start(bf16[256,256]{1,0:T(8,128)(2,1)} %constant.57.clone.bh) | copy-start | bytes 393220
  17.3 28.6 %copy-start.8 = (bf16[256,256]{1,0:T(8,128)(2,1)S(1)}, bf16[256,256]{1,0:T(8,128)(2,1)}, u32[]{:S(2)}) copy-start(bf16[256,256]{1,0:T(8,128)(2,1)} %constant.58.clone.bl) | copy-start | bytes 393220
  17.3 28.6 %copy-start.9 = (f32[16,8,128]{2,1,0:T(8,128)S(1)}, f32[16,8,128]{2,1,0:T(8,128)}, u32[]{:S(2)}) copy-start(f32[16,8,128]{2,1,0:T(8,128)} %constant.59.clone.cos_ref) | copy-start | bytes 196612
  17.3 28.6 %copy-start.10 = (f32[16,8,128]{2,1,0:T(8,128)S(1)}, f32[16,8,128]{2,1,0:T(8,128)}, u32[]{:S(2)}) copy-start(f32[16,8,128]{2,1,0:T(8,128)} %constant.60.clone.sin_ref) | copy-start | bytes 196612
  17.3 28.6 %copy-start.11 = (s32[32]{0:T(128)S(1)}, s32[32]{0:T(128)}, u32[]{:S(2)}) copy-start(s32[32]{0:T(128)} %level_ref.3) | copy-start | bytes 388
  18.0 27.9 %copy-start.4 = (f32[64,3]{1,0:T(8,128)S(1)}, f32[64,3]{1,0:T(8,128)}, u32[]{:S(2)}) copy-start(f32[64,3]{1,0:T(8,128)} %copy.24.table_ref) | copy-start | bytes 2308
  52.4 35.0 %copy-start = (bf16[512,512]{1,0:T(8,128)(2,1)S(1)}, bf16[512,512]{1,0:T(8,128)(2,1)}, u32[]{:S(2)}) copy-start(bf16[512,512]{1,0:T(8,128)(2,1)} %constant.61.clone.eh) | copy-start | bytes 1572868
  52.4 35.0 %copy-start.1 = (bf16[512,512]{1,0:T(8,128)(2,1)S(1)}, bf16[512,512]{1,0:T(8,128)(2,1)}, u32[]{:S(2)}) copy-start(bf16[512,512]{1,0:T(8,128)(2,1)} %constant.62.clone.el) | copy-start | bytes 1572868
  52.4 35.0 %copy-start.2 = (bf16[512,512]{1,0:T(8,128)(2,1)S(1)}, bf16[512,512]{1,0:T(8,128)(2,1)}, u32[]{:S(2)}) copy-start(bf16[512,512]{1,0:T(8,128)(2,1)} %constant.63.clone.oh) | copy-start | bytes 1572868
  52.4 35.0 %copy-start.3 = (bf16[512,512]{1,0:T(8,128)(2,1)S(1)}, bf16[512,512]{1,0:T(8,128)(2,1)}, u32[]{:S(2)}) copy-start(bf16[512,512]{1,0:T(8,128)(2,1)} %constant.64.clone.ol) | copy-start | bytes 1572868

commit v4 on v3

--- a/solution.py
+++ b/solution.py
@@ -16,6 +16,10 @@
 LOCAL = NY // WALLS
 SLAB = NZ // PENS
 ROWS = 2 * OWN
+CLASSES = 4
+SPAN = KX // 2
+OWNERS = DEVICES // CLASSES
+ROOT = np.float32(np.sqrt(0.5))
 MIB = 1 << 20
 F32, BF16 = jnp.float32, jnp.bfloat16
 
@@ -47,19 +51,36 @@
     return high, low.astype(jnp.bfloat16)
 
 
+def class_modes(group, count):
+    if group < 2:
+        return 4 * count + 2 * group
+    return 8 * count + 1 + 4 * (group - 2)
+
+
 def stream_tables():
-    point = np.arange(HALF)
     forward, backward = [], []
-    for odd in (0, 1):
-        mode = 2 * np.arange(KX // 2) + odd
+    for group in range(CLASSES):
+        mode = class_modes(group, np.arange(SPAN // 2))
+        point = np.arange(SPAN if group < 2 else SPAN // 2)
         angle = 2.0 * np.pi * (mode[:, None] * point[None, :] % NX) / NX
-        pair = np.stack([np.cos(angle), -np.sin(angle)], 1)
-        pair = pair.reshape(-1, OWN, 2, HALF).transpose(0, 2, 1, 3).reshape(KX, HALF)
+        cos, sin = np.cos(angle), np.sin(angle)
+        if group < 2:
+            pair = np.stack([cos, -sin], 1)
+        else:
+            mirror = np.where(mode > HALF, -1.0, 1.0)[:, None]
+            pair = np.stack(
+                [
+                    np.concatenate([cos, -sin], 1),
+                    np.concatenate([-sin, -cos], 1) * mirror,
+                ],
+                1,
+            )
+        pair = pair.reshape(-1, OWN, 2, SPAN).transpose(0, 2, 1, 3).reshape(SPAN, SPAN)
         weight = np.where(mode == 0, 1.0, 2.0) / (NX * NZ)
         weight = np.stack([weight, weight], 1).reshape(-1, OWN, 2).transpose(0, 2, 1)
-        forward += halves(pair)
-        backward += halves(pair * weight.reshape(KX, 1))
-    return forward, backward
+        forward.append(halves(pair))
+        backward.append(halves(pair * weight.reshape(SPAN, 1)))
+    return [np.concatenate(sum(pairs, ()), 0) for pairs in (forward, backward)]
 
 
 def span_tables():
@@ -88,47 +109,74 @@
     return jnp.where(top, first, swap(second)), jnp.where(top, swap(first), second)
 
 
-def stream_forward(x_hbm, *refs):
-    tables, out_hbm, x_ref, table_refs, out_ref, x_sem, table_sems, out_sem = (
-        refs[:4], *refs[4:]
-    )
-    owners = DEVICES // 2
+def fold(x):
+    v = [x[:, i * SLAB : (i + 1) * SLAB] for i in range(8)]
+    a = [v[i] + v[i + 4] for i in range(4)]
+    b = [v[i] - v[i + 4] for i in range(4)]
+    p, q = (b[1] - b[3]) * ROOT, (b[1] + b[3]) * ROOT
+    return [
+        jnp.concatenate(pair, 1)
+        for pair in (
+            (a[0] + a[2], a[1] + a[3]),
+            (a[0] - a[2], a[1] - a[3]),
+            (b[0] + p, b[2] + q),
+            (b[0] - p, b[2] - q),
+        )
+    ]
+
+
+def unfold(sums):
+    (a0, a1), (b0, b1), (c0, c1), (d0, d1) = ((s[:, :SLAB], s[:, SLAB:]) for s in sums)
+    a = [a0 + b0, a1 + b1, a0 - b0, a1 - b1]
+    p, q = (c0 - d0) * ROOT, (c1 - d1) * ROOT
+    b = [c0 + d0, q + p, c1 + d1, q - p]
+    return [u + v for u, v in zip(a, b)] + [u - v for u, v in zip(a, b)]
+
+
+def stream_forward(x_hbm, table_hbm, out_hbm, x_ref, table_ref, out_ref, x_sem, table_sem, out_sem):
     pairs = LOCAL // 2
-    loads = [
+
+    def part(i):
+        return slice(2 * SPAN * i, 2 * SPAN * (i + 1))
+
+    x_loads = [
         pltpu.make_async_copy(x_hbm.at[2 * i : 2 * i + 2], x_ref.at[2 * i : 2 * i + 2], x_sem.at[i])
         for i in range(pairs)
     ]
     table_loads = [
-        pltpu.make_async_copy(tables[i], table_refs.at[i], table_sems.at[i]) for i in range(4)
+        pltpu.make_async_copy(table_hbm.at[part(i)], table_ref.at[part(i)], table_sem.at[i])
+        for i in range(CLASSES)
     ]
-    loads[0].start()
-    for load in table_loads + loads[1:]:
+    for load in x_loads[:1] + table_loads + x_loads[1:]:
         load.start()
     dot = functools.partial(
         lax.dot_general, dimension_numbers=(((1,), (1,)), ((), ())), preferred_element_type=F32
     )
     stores = []
     for i in range(pairs):
-        loads[i].wait()
-        x = x_ref[2 * i : 2 * i + 2].reshape(2 * SLAB, NX)
-        first, second = x[:, :HALF], x[:, HALF:]
-        for odd, value in enumerate((first + second, first - second)):
+        x_loads[i].wait()
+        folded = fold(x_ref[2 * i : 2 * i + 2].reshape(2 * SLAB, NX))
+        for group, value in enumerate(folded):
             if i == 0:
-                table_loads[2 * odd].wait()
-                table_loads[2 * odd + 1].wait()
+                table_loads[group].wait()
             high, low = split(value)
-            table = table_refs[2 * odd]
-            got = dot(table, high) + dot(table, low) + dot(table_refs[2 * odd + 1], high)
-            base = odd * owners
+            start = 2 * SPAN * group
+            table = table_ref[start : start + SPAN]
+            got = (
+                dot(table, high)
+                + dot(table, low)
+                + dot(table_ref[start + SPAN : start + 2 * SPAN], high)
+            )
             parts = exchange_rows(
-                *(got[:, j * SLAB : (j + 1) * SLAB].reshape(owners, ROWS, SLAB) for j in (0, 1))
+                *(got[:, j * SLAB : (j + 1) * SLAB].reshape(OWNERS, ROWS, SLAB) for j in (0, 1))
             )
-            for part in (0, 1):
-                out_ref[base : base + owners, i, part] = parts[part]
-            region = (slice(base, base + owners), i)
+            base = group * OWNERS
+            for k in (0, 1):
+                out_ref[base : base + OWNERS, i, k] = parts[k]
+            region = (slice(base, base + OWNERS), i)
             stores.append(
                 pltpu.make_async_copy(
-                    out_ref.at[region], out_hbm.at[region], out_sem.at[2 * i + odd]
+                    out_ref.at[region], out_hbm.at[region], out_sem.at[CLASSES * i + group]
                 )
             )
             stores[-1].start()
@@ -136,19 +184,22 @@
         store.wait()
 
 
-def stream_backward(y_ref, eh, el, oh, ol, out_ref):
-    owners = DEVICES // 2
+def stream_backward(y_ref, table_ref, out_ref):
     dot = functools.partial(jnp.dot, preferred_element_type=F32)
     sums = []
-    for high_ref, low_ref, base in ((eh, el, 0), (oh, ol, owners)):
-        planes = exchange_rows(*(y_ref[base : base + owners, 0, part] for part in (0, 1)))
-        value = jnp.concatenate([plane.reshape(KX, SLAB).T for plane in planes], 0)
+    for group in range(CLASSES):
+        base, start = group * OWNERS, 2 * SPAN * group
+        planes = exchange_rows(*(y_ref[base : base + OWNERS, 0, k] for k in (0, 1)))
+        value = jnp.concatenate([plane.reshape(SPAN, SLAB).T for plane in planes], 0)
         high, low = split(value)
-        table = high_ref[...]
-        sums.append(dot(high, table) + dot(low, table) + dot(high, low_ref[...]))
-    even, odd = sums
-    out_ref[:, :, :HALF] = (even + odd).reshape(2, SLAB, HALF)
-    out_ref[:, :, HALF:] = (even - odd).reshape(2, SLAB, HALF)
+        table = table_ref[start : start + SPAN]
+        sums.append(
+            dot(high, table)
+            + dot(low, table)
+            + dot(high, table_ref[start + SPAN : start + 2 * SPAN])
+        )
+    for i, value in enumerate(unfold(sums)):
+        out_ref[:, :, i * SLAB : (i + 1) * SLAB] = value.reshape(2, SLAB, SLAB)
 
 
 def modified(index, length):
@@ -159,13 +210,16 @@
     place_ref, table_ref, level_ref, stream_ref, span_ref, out_hbm, inverse_ref, sem
 ):
     place = place_ref[0]
-    owners = DEVICES // 2
-    odd = place // owners
-    start = 2 * OWN * (place % owners) + odd
+    group, first = place // OWNERS, OWN * (place % OWNERS)
     row = lax.broadcasted_iota(jnp.int32, (ROWS, 128), 0) % OWN
     wave = jnp.zeros((ROWS, 128), jnp.int32)
     for i in range(OWN):
-        wave = jnp.where(row == i, stream_ref[start + 2 * i], wave)
+        count = first + i
+        mode = jnp.where(
+            group < 2, 4 * count + 2 * group, 8 * count + 1 + 4 * (group - 2)
+        )
+        mode = jnp.where(mode > HALF, NX - mode, mode)
+        wave = jnp.where(row == i, stream_ref[mode], wave)
     wave_x = modified(wave, NX)
     wave_z = modified(span_ref[...], NZ)
     squared = wave_x[None] + wave_z[:, None, :]
@@ -327,31 +381,28 @@
 VMEM = pl.BlockSpec(memory_space=pltpu.VMEM)
 SMEM = pl.BlockSpec(memory_space=pltpu.SMEM)
 HBM = pl.BlockSpec(memory_space=pltpu.HBM)
-STEP = 2
 
 
 def on_device(right_side, coef_table, stretch_index, stream_wave, span_wave):
     forward, backward = stream_tables()
     chunks = jax.ShapeDtypeStruct((DEVICES, LOCAL // 2, 2, ROWS, SLAB), F32)
-    fixed = pl.BlockSpec((KX, HALF), lambda i: (0, 0))
     chunk_spec = pl.BlockSpec((DEVICES, 1, 2, ROWS, SLAB), lambda i: (0, i, 0, 0, 0))
-    field_spec = pl.BlockSpec((STEP, SLAB, NX), lambda i: (i, 0, 0))
     spectra = pl.pallas_call(
         stream_forward,
-        in_specs=[HBM] * 5,
+        in_specs=[HBM] * 2,
         out_specs=HBM,
         out_shape=chunks,
         scratch_shapes=[
             pltpu.VMEM((LOCAL, SLAB, NX), F32),
-            pltpu.VMEM((4, KX, HALF), BF16),
+            pltpu.VMEM(forward.shape, BF16),
             pltpu.VMEM(chunks.shape, F32),
             pltpu.SemaphoreType.DMA((LOCAL // 2,)),
-            pltpu.SemaphoreType.DMA((4,)),
-            pltpu.SemaphoreType.DMA((LOCAL,)),
+            pltpu.SemaphoreType.DMA((CLASSES,)),
+            pltpu.SemaphoreType.DMA((LOCAL // 2 * CLASSES,)),
         ],
         compiler_params=params(60),
         name="stream_forward",
-    )(right_side, *forward)
+    )(right_side, forward)
     place = sum(lax.axis_index(n) * s for n, s in strides().items()).reshape(1)
     inverse = pl.pallas_call(
         divisors,
@@ -377,13 +428,13 @@
     solved = lax.all_to_all(solved, ORDER, 0, 0, tiled=True)
     return pl.pallas_call(
         stream_backward,
-        grid=(LOCAL // STEP,),
-        in_specs=[chunk_spec] + [fixed] * 4,
-        out_specs=field_spec,
+        grid=(LOCAL // 2,),
+        in_specs=[chunk_spec, pl.BlockSpec(backward.shape, lambda i: (0, 0))],
+        out_specs=pl.BlockSpec((2, SLAB, NX), lambda i: (i, 0, 0)),
         out_shape=jax.ShapeDtypeStruct(right_side.shape, F32),
         compiler_params=params(40),
         name="stream_backward",
-    )(solved, *backward)
+    )(solved, backward)
 
 
 def solution(mesh):

time: 91.2 us -> 89.5 us (0.981)
  Pallas kernels: 18.9 us -> 17.2 us
    pallas_call x2, Pallas kernels: 8.9 us -> 7.29 us  [the longest x1 4.7 us: on_device(): pl.pallas_call(stream_forward, in_specs=[HBM] * 2, out_specs=HBM, out_sha...]
where the time goes in v4:
time: 89.5 us; the launch traced here: 88.9 us
  blocking collectives  34.9 us (39%)
  waiting for transfers between devices  23.5 us (26%)
  Pallas kernels  17.2 us (19%)
  starting transfers between devices  11.5 us (13%)
  local copies, waits for them, and re-layouts  1.52 us (2%)
    all_to_all x1, blocking collectives, on_device(): solved = lax.all_to_all(solved, ORDER, 0, 0, tiled=True)  34.9 us
    all_to_all x1, waiting for transfers between devices, on_device(): spectra = lax.all_to_all(spectra, ORDER, 0, 0, tiled=True)  23.5 us
    all_to_all x1, starting transfers between devices, on_device(): spectra = lax.all_to_all(spectra, ORDER, 0, 0, tiled=True)  11.5 us
    pallas_call x1, Pallas kernels, on_device(): pl.pallas_call(span_solve, in_specs=[SMEM] * 2 + [VMEM, HBM] + [VMEM] * 6...  6.45 us
    pallas_call x1, Pallas kernels, on_device(): pl.pallas_call(stream_forward, in_specs=[HBM] * 2, out_specs=HBM, out_sha...  4.7 us
    pallas_call x1, Pallas kernels, on_device(): pl.pallas_call(divisors, in_specs=[SMEM] * 4 + [VMEM], out_specs=HBM, out...  3.51 us
    pallas_call x1, Pallas kernels, on_device(): pl.pallas_call(stream_backward, grid=(LOCAL // 2,), in_specs=[chunk_spec,...  2.59 us
  transfers between devices with their start and end apart: 1, of which 1 were waited for; matrix products, arithmetic and copies ran while one was open for 2% of the time, Pallas kernels for 4%

profile of v4, /device:TPU:1, one launch (start us, length us, event | category | flops | bytes accessed | tf_op | source)
XLA Modules:
  0.0 88.9 jit_solution(5227381675650428293)
XLA Ops:
  0.0 4.7 %stream_forward.1 = f32[128,2,2,8,128]{4,3,2,1,0:T(8,128)} custom-call(f32[4,128,1024]{2,1,0:T(8,128)} %x_hbm.1, bf16[2048,256]{1,0:T(8,128)(2,1)} %constant.39.clone.table_hbm), custom_call_target="tpu_custom_call" | custom-call | tf_op jit(solution)/shard_map/stream_forward/pallas_call | solution.py:390
  4.7 0.0 copy-start.10
  4.7 0.0 copy-start.9
  4.7 11.5 %all-to-all-start = ((f32[128,2,2,8,128]{4,3,2,1,0:T(8,128)}), f32[128,2,2,8,128]{4,3,2,1,0:T(8,128)S(1)}, u32[]{:S(2)}, u32[]{:S(2)}) async-start(f32[128,2,2,8,128]{4,3,2,1,0:T(8,128)} %stream_forward.1), calls=%async_computation | async-start | bytes 4194304 | tf_op jit(solution)/shard_map/all_to_all | solution.py:417
  16.2 0.0 copy-start.2
  16.3 0.0 copy-start.3
  16.3 0.0 copy-start.4
  16.3 0.0 copy-start.5
  16.3 0.0 copy-start.6
  16.3 0.0 copy-start.7
  16.3 0.0 copy-start.8
  16.3 0.0 copy-done.10
  16.3 0.7 copy.18.table_ref
  17.0 0.0 copy-done.9
  17.1 0.1 reshape.7
  17.1 0.7 copy.16
  17.8 3.5 %divisors.1.inverse_hbm = f32[32,16,8,128]{3,2,1,0:T(8,128)} custom-call(s32[1]{0:T(128)} %bitcast.place_ref, f32[64,3]{1,0:T(8,128)} %copy.18.table_ref, s32[32]{0:T(128)} %level_ref.3, s32[512]{0:T(512)} %stream_ref.1, s32[16,128]{1,0:T(8,128)} %bitcast.2), custom_call_target="tpu_custom_call" | custom-call | flops 10000000 | bytes 2097152 | tf_op jit(solution)/shard_map/divisors/pallas_call | solution.py:407
  21.3 23.5 %all-to-all-done.in_ref = f32[128,2,2,8,128]{4,3,2,1,0:T(8,128)S(1)} async-done(((f32[128,2,2,8,128]{4,3,2,1,0:T(8,128)}), f32[128,2,2,8,128]{4,3,2,1,0:T(8,128)S(1)}, u32[]{:S(2)}, u32[]{:S(2)}) %all-to-all-start) | async-done | bytes 2097184 | tf_op jit(solution)/shard_map/all_to_all | solution.py:417
  44.8 0.0 copy-done.2
  44.8 0.0 copy-done.3
  44.9 6.5 %span_solve.1 = f32[128,2,2,8,128]{4,3,2,1,0:T(8,128)S(1)} custom-call(f32[64,3]{1,0:T(8,128)S(1)} %copy-done.1, s32[32]{0:T(128)S(1)} %copy-done.8, f32[128,2,2,8,128]{4,3,2,1,0:T(8,128)S(1)} %all-to-all-done.in_ref, f32[32,16,8,128]{3,2,1,0:T(8,128)} %divisors.1.inverse_hbm, bf16[256,256]{1,0:T(8,128)(2,1)S(1)} %copy-done.2, ...), custom_call_target="tpu_custom_call" | custom-call | tf_op jit(solution)/shard_map/span_solve/pallas_call | solution.py:418
  51.4 0.0 copy-start
  51.4 34.9 %all_to_all.10.y_ref = f32[128,2,2,8,128]{4,3,2,1,0:T(8,128)S(1)} all-to-all(f32[128,2,2,8,128]{4,3,2,1,0:T(8,128)S(1)} %span_solve.1), channel_id=1, replica_groups=mesh['x'=4,'core'=2,'z'=4,'y'=4] {'core','x','y','z'}, dimensions={0} | all-to-all | bytes 4194304 | tf_op jit(solution)/shard_map/all_to_all | solution.py:428
  86.3 2.6 %stream_backward.1 = f32[4,128,1024]{2,1,0:T(8,128)} custom-call(f32[128,2,2,8,128]{4,3,2,1,0:T(8,128)S(1)} %all_to_all.10.y_ref, bf16[2048,256]{1,0:T(8,128)(2,1)S(1)} %copy-done), custom_call_target="tpu_custom_call" | custom-call | tf_op jit(solution)/shard_map/stream_backward/pallas_call | solution.py:429
  (8 shorter events, 0.0 us)
Async XLA Ops:
  4.7 11.6 %copy-start.10 = (f32[64,3]{0,1:T(4,128)S(1)}, f32[64,3]{0,1:T(4,128)}, u32[]{:S(2)}) copy-start(f32[64,3]{0,1:T(4,128)} %param.14) | copy-start | bytes 2308
  4.7 12.3 %copy-start.9 = (s32[2048]{0:T(1024)S(1)}, s32[2048]{0:T(1024)}, u32[]{:S(2)}) copy-start(s32[2048]{0:T(1024)} %param.17) | copy-start | bytes 24580
  4.7 40.1 %all-to-all-start = ((f32[128,2,2,8,128]{4,3,2,1,0:T(8,128)}), f32[128,2,2,8,128]{4,3,2,1,0:T(8,128)S(1)}, u32[]{:S(2)}, u32[]{:S(2)}) async-start(f32[128,2,2,8,128]{4,3,2,1,0:T(8,128)} %stream_forward.1), calls=%async_computation | async-start | bytes 4194304 | tf_op jit(solution)/shard_map/all_to_all | solution.py:417
  16.2 28.6 %copy-start.2 = (bf16[256,256]{1,0:T(8,128)(2,1)S(1)}, bf16[256,256]{1,0:T(8,128)(2,1)}, u32[]{:S(2)}) copy-start(bf16[256,256]{1,0:T(8,128)(2,1)} %constant.40.clone.fh) | copy-start | bytes 393220
  16.3 28.6 %copy-start.3 = (bf16[256,256]{1,0:T(8,128)(2,1)S(1)}, bf16[256,256]{1,0:T(8,128)(2,1)}, u32[]{:S(2)}) copy-start(bf16[256,256]{1,0:T(8,128)(2,1)} %constant.41.clone.fl) | copy-start | bytes 393220
  16.3 28.6 %copy-start.4 = (bf16[256,256]{1,0:T(8,128)(2,1)S(1)}, bf16[256,256]{1,0:T(8,128)(2,1)}, u32[]{:S(2)}) copy-start(bf16[256,256]{1,0:T(8,128)(2,1)} %constant.42.clone.bh) | copy-start | bytes 393220
  16.3 28.6 %copy-start.5 = (bf16[256,256]{1,0:T(8,128)(2,1)S(1)}, bf16[256,256]{1,0:T(8,128)(2,1)}, u32[]{:S(2)}) copy-start(bf16[256,256]{1,0:T(8,128)(2,1)} %constant.43.clone.bl) | copy-start | bytes 393220
  16.3 28.6 %copy-start.6 = (f32[16,8,128]{2,1,0:T(8,128)S(1)}, f32[16,8,128]{2,1,0:T(8,128)}, u32[]{:S(2)}) copy-start(f32[16,8,128]{2,1,0:T(8,128)} %constant.44.clone.cos_ref) | copy-start | bytes 196612
  16.3 28.6 %copy-start.7 = (f32[16,8,128]{2,1,0:T(8,128)S(1)}, f32[16,8,128]{2,1,0:T(8,128)}, u32[]{:S(2)}) copy-start(f32[16,8,128]{2,1,0:T(8,128)} %constant.45.clone.sin_ref) | copy-start | bytes 196612
  16.3 28.6 %copy-start.8 = (s32[32]{0:T(128)S(1)}, s32[32]{0:T(128)}, u32[]{:S(2)}) copy-start(s32[32]{0:T(128)} %level_ref.3) | copy-start | bytes 388
  17.0 27.8 %copy-start.1 = (f32[64,3]{1,0:T(8,128)S(1)}, f32[64,3]{1,0:T(8,128)}, u32[]{:S(2)}) copy-start(f32[64,3]{1,0:T(8,128)} %copy.18.table_ref) | copy-start | bytes 2308
  51.4 34.9 %copy-start = (bf16[2048,256]{1,0:T(8,128)(2,1)S(1)}, bf16[2048,256]{1,0:T(8,128)(2,1)}, u32[]{:S(2)}) copy-start(bf16[2048,256]{1,0:T(8,128)(2,1)} %constant.46.clone.table_ref) | copy-start | bytes 3145732

commit v5 on v4

--- a/solution.py
+++ b/solution.py
@@ -153,30 +153,31 @@
         lax.dot_general, dimension_numbers=(((1,), (1,)), ((), ())), preferred_element_type=F32
     )
     stores = []
+    for load in table_loads:
+        load.wait()
     for i in range(pairs):
         x_loads[i].wait()
         folded = fold(x_ref[2 * i : 2 * i + 2].reshape(2 * SLAB, NX))
-        for group, value in enumerate(folded):
-            if i == 0:
-                table_loads[group].wait()
-            high, low = split(value)
-            start = 2 * SPAN * group
-            table = table_ref[start : start + SPAN]
-            got = (
-                dot(table, high)
-                + dot(table, low)
-                + dot(table_ref[start + SPAN : start + 2 * SPAN], high)
-            )
-            parts = exchange_rows(
-                *(got[:, j * SLAB : (j + 1) * SLAB].reshape(OWNERS, ROWS, SLAB) for j in (0, 1))
-            )
-            base = group * OWNERS
-            for k in (0, 1):
-                out_ref[base : base + OWNERS, i, k] = parts[k]
-            region = (slice(base, base + OWNERS), i)
+        for members in (((0,1,2,3),),((0,1),(2,3)))[i]:
+            for group in members:
+                high, low = split(folded[group])
+                start = 2 * SPAN * group
+                table = table_ref[start : start + SPAN]
+                got = (
+                    dot(table, high)
+                    + dot(table, low)
+                    + dot(table_ref[start + SPAN : start + 2 * SPAN], high)
+                )
+                parts = exchange_rows(
+                    *(got[:, j * SLAB : (j + 1) * SLAB].reshape(OWNERS, ROWS, SLAB) for j in (0, 1))
+                )
+                base = group * OWNERS
+                for k in (0, 1):
+                    out_ref[base : base + OWNERS, i, k] = parts[k]
+            region = (slice(members[0] * OWNERS, (members[-1] + 1) * OWNERS), i)
             stores.append(
                 pltpu.make_async_copy(
-                    out_ref.at[region], out_hbm.at[region], out_sem.at[CLASSES * i + group]
+                    out_ref.at[region], out_hbm.at[region], out_sem.at[len(stores)]
                 )
             )
             stores[-1].start()
@@ -184,22 +185,35 @@
         store.wait()
 
 
-def stream_backward(y_ref, table_ref, out_ref):
+def stream_backward(y_ref, table_ref, out_hbm, out_ref, sem):
     dot = functools.partial(jnp.dot, preferred_element_type=F32)
-    sums = []
-    for group in range(CLASSES):
-        base, start = group * OWNERS, 2 * SPAN * group
-        planes = exchange_rows(*(y_ref[base : base + OWNERS, 0, k] for k in (0, 1)))
-        value = jnp.concatenate([plane.reshape(SPAN, SLAB).T for plane in planes], 0)
-        high, low = split(value)
-        table = table_ref[start : start + SPAN]
-        sums.append(
-            dot(high, table)
-            + dot(low, table)
-            + dot(high, table_ref[start + SPAN : start + 2 * SPAN])
-        )
-    for i, value in enumerate(unfold(sums)):
-        out_ref[:, :, i * SLAB : (i + 1) * SLAB] = value.reshape(2, SLAB, SLAB)
+    stores = []
+    for i in range(LOCAL // 2):
+        planes = [
+            exchange_rows(*(y_ref[g * OWNERS : (g + 1) * OWNERS, i, k] for k in (0, 1)))
+            for g in range(CLASSES)
+        ]
+        for j in (0, 1):
+            sums = []
+            for group in range(CLASSES):
+                start = 2 * SPAN * group
+                high, low = split(planes[group][j].reshape(SPAN, SLAB).T)
+                table = table_ref[start : start + SPAN]
+                sums.append(
+                    dot(high, table)
+                    + dot(low, table)
+                    + dot(high, table_ref[start + SPAN : start + 2 * SPAN])
+                )
+            for k, value in enumerate(unfold(sums)):
+                out_ref[2 * i + j, :, k * SLAB : (k + 1) * SLAB] = value
+            stores.append(
+                pltpu.make_async_copy(
+                    out_ref.at[2 * i + j], out_hbm.at[2 * i + j], sem.at[2 * i + j]
+                )
+            )
+            stores[-1].start()
+    for store in stores:
+        store.wait()
 
 
 def modified(index, length):
@@ -314,7 +328,9 @@
 
     def eliminate(w, got, before):
         got = got.reshape(pairs, PENS, ROWS, 2 * SLAB)
-        loads[w].wait()
+        if w == 0:
+            for load in loads:
+                load.wait()
         for i in range(pairs):
             planes = exchange_rows(got[i, :, :, :SLAB], got[i, :, :, SLAB:])
             for j, source in enumerate(planes):
@@ -359,12 +375,10 @@
                     out_ref[base + pen_offset(p), i, part] = value[part]
 
     high, low = fh[...], fl[...]
-    parts, before = gather(0), None
+    spectra = [span_dot(gather(w), high, low) for w in range(WALLS)]
+    before = None
     for w in range(WALLS):
-        got = span_dot(parts, high, low)
-        if w + 1 < WALLS:
-            parts = gather(w + 1)
-        before = eliminate(w, got, before)
+        before = eliminate(w, spectra[w], before)
     high, low = bh[...], bl[...]
     after, parts = substitute(WALLS - 1, None)
     for w in reversed(range(WALLS)):
@@ -386,7 +400,6 @@
 def on_device(right_side, coef_table, stretch_index, stream_wave, span_wave):
     forward, backward = stream_tables()
     chunks = jax.ShapeDtypeStruct((DEVICES, LOCAL // 2, 2, ROWS, SLAB), F32)
-    chunk_spec = pl.BlockSpec((DEVICES, 1, 2, ROWS, SLAB), lambda i: (0, i, 0, 0, 0))
     spectra = pl.pallas_call(
         stream_forward,
         in_specs=[HBM] * 2,
@@ -428,10 +441,13 @@
     solved = lax.all_to_all(solved, ORDER, 0, 0, tiled=True)
     return pl.pallas_call(
         stream_backward,
-        grid=(LOCAL // 2,),
-        in_specs=[chunk_spec, pl.BlockSpec(backward.shape, lambda i: (0, 0))],
-        out_specs=pl.BlockSpec((2, SLAB, NX), lambda i: (i, 0, 0)),
+        in_specs=[VMEM] * 2,
+        out_specs=HBM,
         out_shape=jax.ShapeDtypeStruct(right_side.shape, F32),
+        scratch_shapes=[
+            pltpu.VMEM(right_side.shape, F32),
+            pltpu.SemaphoreType.DMA((LOCAL,)),
+        ],
         compiler_params=params(40),
         name="stream_backward",
     )(solved, backward)

time: 89.5 us -> 87 us (0.972)
  Pallas kernels: 17.2 us -> 14.7 us
    pallas_call x1, Pallas kernels: 6.45 us -> 5.45 us  [on_device(): pl.pallas_call(span_solve, in_specs=[SMEM] * 2 + [VMEM, HBM] + [VMEM] * 6...]
    pallas_call x1, Pallas kernels: 4.7 us -> 3.73 us  [on_device(): pl.pallas_call(stream_forward, in_specs=[HBM] * 2, out_specs=HBM, out_sha...]
where the time goes in v5:
time: 87 us; the launch traced here: 86.3 us
  blocking collectives  34.9 us (40%)
  waiting for transfers between devices  23.5 us (27%)
  Pallas kernels  14.7 us (17%)
  starting transfers between devices  11.5 us (13%)
  local copies, waits for them, and re-layouts  1.52 us (2%)
    all_to_all x1, blocking collectives, on_device(): solved = lax.all_to_all(solved, ORDER, 0, 0, tiled=True)  34.9 us
    all_to_all x1, waiting for transfers between devices, on_device(): spectra = lax.all_to_all(spectra, ORDER, 0, 0, tiled=True)  23.5 us
    all_to_all x1, starting transfers between devices, on_device(): spectra = lax.all_to_all(spectra, ORDER, 0, 0, tiled=True)  11.5 us
    pallas_call x1, Pallas kernels, on_device(): pl.pallas_call(span_solve, in_specs=[SMEM] * 2 + [VMEM, HBM] + [VMEM] * 6...  5.45 us
    pallas_call x1, Pallas kernels, on_device(): pl.pallas_call(stream_forward, in_specs=[HBM] * 2, out_specs=HBM, out_sha...  3.73 us
    pallas_call x1, Pallas kernels, on_device(): pl.pallas_call(divisors, in_specs=[SMEM] * 4 + [VMEM], out_specs=HBM, out...  3.51 us
    pallas_call x1, Pallas kernels, on_device(): pl.pallas_call(stream_backward, in_specs=[VMEM] * 2, out_specs=HBM, out_s...  1.98 us
  transfers between devices with their start and end apart: 1, of which 1 were waited for; matrix products, arithmetic and copies ran while one was open for 2% of the time, Pallas kernels for 4%

profile of v5, /device:TPU:1, one launch (start us, length us, event | category | flops | bytes accessed | tf_op | source)
XLA Modules:
  0.0 86.3 jit_solution(10002738485318739063)
XLA Ops:
  0.0 3.7 %stream_forward.1 = f32[128,2,2,8,128]{4,3,2,1,0:T(8,128)} custom-call(f32[4,128,1024]{2,1,0:T(8,128)} %x_hbm.1, bf16[2048,256]{1,0:T(8,128)(2,1)} %constant.39.clone.table_hbm), custom_call_target="tpu_custom_call" | custom-call | tf_op jit(solution)/shard_map/stream_forward/pallas_call | solution.py:403
  3.7 0.0 copy-start.10
  3.7 0.0 copy-start.9
  3.8 11.5 %all-to-all-start = ((f32[128,2,2,8,128]{4,3,2,1,0:T(8,128)}), f32[128,2,2,8,128]{4,3,2,1,0:T(8,128)S(1)}, u32[]{:S(2)}, u32[]{:S(2)}) async-start(f32[128,2,2,8,128]{4,3,2,1,0:T(8,128)} %stream_forward.1), calls=%async_computation | async-start | bytes 4194304 | tf_op jit(solution)/shard_map/all_to_all | solution.py:430
  15.3 0.0 copy-start.2
  15.3 0.0 copy-start.3
  15.3 0.0 copy-start.4
  15.3 0.0 copy-start.5
  15.3 0.0 copy-start.6
  15.3 0.0 copy-start.7
  15.3 0.0 copy-start.8
  15.4 0.7 copy.18.table_ref
  16.1 0.1 reshape.7
  16.2 0.7 copy.16
  16.8 3.5 %divisors.1.inverse_hbm = f32[32,16,8,128]{3,2,1,0:T(8,128)} custom-call(s32[1]{0:T(128)} %bitcast.place_ref, f32[64,3]{1,0:T(8,128)} %copy.18.table_ref, s32[32]{0:T(128)} %level_ref.3, s32[512]{0:T(512)} %stream_ref.1, s32[16,128]{1,0:T(8,128)} %bitcast.2), custom_call_target="tpu_custom_call" | custom-call | flops 10000000 | bytes 2097152 | tf_op jit(solution)/shard_map/divisors/pallas_call | solution.py:420
  20.3 23.5 %all-to-all-done.in_ref = f32[128,2,2,8,128]{4,3,2,1,0:T(8,128)S(1)} async-done(((f32[128,2,2,8,128]{4,3,2,1,0:T(8,128)}), f32[128,2,2,8,128]{4,3,2,1,0:T(8,128)S(1)}, u32[]{:S(2)}, u32[]{:S(2)}) %all-to-all-start) | async-done | bytes 2097184 | tf_op jit(solution)/shard_map/all_to_all | solution.py:430
  43.9 0.0 copy-done.5
  43.9 0.0 copy-done.6
  43.9 0.0 copy-done.7
  43.9 0.0 copy-done.8
  43.9 5.5 %span_solve.1 = f32[128,2,2,8,128]{4,3,2,1,0:T(8,128)S(1)} custom-call(f32[64,3]{1,0:T(8,128)S(1)} %copy-done.1, s32[32]{0:T(128)S(1)} %copy-done.8, f32[128,2,2,8,128]{4,3,2,1,0:T(8,128)S(1)} %all-to-all-done.in_ref, f32[32,16,8,128]{3,2,1,0:T(8,128)} %divisors.1.inverse_hbm, bf16[256,256]{1,0:T(8,128)(2,1)S(1)} %copy-done.2, ...), custom_call_target="tpu_custom_call" | custom-call | tf_op jit(solution)/shard_map/span_solve/pallas_call | solution.py:431
  49.4 0.0 copy-start
  49.4 34.9 %all_to_all.10.y_ref = f32[128,2,2,8,128]{4,3,2,1,0:T(8,128)S(1)} all-to-all(f32[128,2,2,8,128]{4,3,2,1,0:T(8,128)S(1)} %span_solve.1), channel_id=1, replica_groups=mesh['x'=4,'core'=2,'z'=4,'y'=4] {'core','x','y','z'}, dimensions={0} | all-to-all | bytes 4194304 | tf_op jit(solution)/shard_map/all_to_all | solution.py:441
  84.3 2.0 %stream_backward.1 = f32[4,128,1024]{2,1,0:T(8,128)} custom-call(f32[128,2,2,8,128]{4,3,2,1,0:T(8,128)S(1)} %all_to_all.10.y_ref, bf16[2048,256]{1,0:T(8,128)(2,1)S(1)} %copy-done), custom_call_target="tpu_custom_call" | custom-call | tf_op jit(solution)/shard_map/stream_backward/pallas_call | solution.py:442
  (8 shorter events, 0.0 us)
Async XLA Ops:
  3.7 11.6 %copy-start.10 = (f32[64,3]{0,1:T(4,128)S(1)}, f32[64,3]{0,1:T(4,128)}, u32[]{:S(2)}) copy-start(f32[64,3]{0,1:T(4,128)} %param.14) | copy-start | bytes 2308
  3.7 12.3 %copy-start.9 = (s32[2048]{0:T(1024)S(1)}, s32[2048]{0:T(1024)}, u32[]{:S(2)}) copy-start(s32[2048]{0:T(1024)} %param.17) | copy-start | bytes 24580
  3.8 40.1 %all-to-all-start = ((f32[128,2,2,8,128]{4,3,2,1,0:T(8,128)}), f32[128,2,2,8,128]{4,3,2,1,0:T(8,128)S(1)}, u32[]{:S(2)}, u32[]{:S(2)}) async-start(f32[128,2,2,8,128]{4,3,2,1,0:T(8,128)} %stream_forward.1), calls=%async_computation | async-start | bytes 4194304 | tf_op jit(solution)/shard_map/all_to_all | solution.py:430
  15.3 28.6 %copy-start.2 = (bf16[256,256]{1,0:T(8,128)(2,1)S(1)}, bf16[256,256]{1,0:T(8,128)(2,1)}, u32[]{:S(2)}) copy-start(bf16[256,256]{1,0:T(8,128)(2,1)} %constant.40.clone.fh) | copy-start | bytes 393220
  15.3 28.6 %copy-start.3 = (bf16[256,256]{1,0:T(8,128)(2,1)S(1)}, bf16[256,256]{1,0:T(8,128)(2,1)}, u32[]{:S(2)}) copy-start(bf16[256,256]{1,0:T(8,128)(2,1)} %constant.41.clone.fl) | copy-start | bytes 393220
  15.3 28.6 %copy-start.4 = (bf16[256,256]{1,0:T(8,128)(2,1)S(1)}, bf16[256,256]{1,0:T(8,128)(2,1)}, u32[]{:S(2)}) copy-start(bf16[256,256]{1,0:T(8,128)(2,1)} %constant.42.clone.bh) | copy-start | bytes 393220
  15.3 28.6 %copy-start.5 = (bf16[256,256]{1,0:T(8,128)(2,1)S(1)}, bf16[256,256]{1,0:T(8,128)(2,1)}, u32[]{:S(2)}) copy-start(bf16[256,256]{1,0:T(8,128)(2,1)} %constant.43.clone.bl) | copy-start | bytes 393220
  15.3 28.6 %copy-start.6 = (f32[16,8,128]{2,1,0:T(8,128)S(1)}, f32[16,8,128]{2,1,0:T(8,128)}, u32[]{:S(2)}) copy-start(f32[16,8,128]{2,1,0:T(8,128)} %constant.44.clone.cos_ref) | copy-start | bytes 196612
  15.3 28.6 %copy-start.7 = (f32[16,8,128]{2,1,0:T(8,128)S(1)}, f32[16,8,128]{2,1,0:T(8,128)}, u32[]{:S(2)}) copy-start(f32[16,8,128]{2,1,0:T(8,128)} %constant.45.clone.sin_ref) | copy-start | bytes 196612
  15.3 28.6 %copy-start.8 = (s32[32]{0:T(128)S(1)}, s32[32]{0:T(128)}, u32[]{:S(2)}) copy-start(s32[32]{0:T(128)} %level_ref.3) | copy-start | bytes 388
  16.1 27.8 %copy-start.1 = (f32[64,3]{1,0:T(8,128)S(1)}, f32[64,3]{1,0:T(8,128)}, u32[]{:S(2)}) copy-start(f32[64,3]{1,0:T(8,128)} %copy.18.table_ref) | copy-start | bytes 2308
  49.4 34.9 %copy-start = (bf16[2048,256]{1,0:T(8,128)(2,1)S(1)}, bf16[2048,256]{1,0:T(8,128)(2,1)}, u32[]{:S(2)}) copy-start(bf16[2048,256]{1,0:T(8,128)(2,1)} %constant.46.clone.table_ref) | copy-start | bytes 3145732

commit v6 on v5

--- a/solution.py
+++ b/solution.py
@@ -19,6 +19,7 @@
 CLASSES = 4
 SPAN = KX // 2
 OWNERS = DEVICES // CLASSES
+SPARE = 8
 ROOT = np.float32(np.sqrt(0.5))
 MIB = 1 << 20
 F32, BF16 = jnp.float32, jnp.bfloat16
@@ -247,7 +248,7 @@
         return upper * inverse
 
     lax.fori_loop(0, NY, step, jnp.zeros((PENS, ROWS, 128), F32))
-    store = pltpu.make_async_copy(inverse_ref, out_hbm, sem)
+    store = pltpu.make_async_copy(inverse_ref, out_hbm.at[:NY], sem)
     store.start()
     store.wait()
 
@@ -297,16 +298,11 @@
 
 def span_solve(
     table_ref, level_ref, in_ref, inverse_hbm, fh, fl, bh, bl, cos_ref, sin_ref,
-    out_ref, held_ref, inverse_ref, sems,
+    out_ref, held_ref, inverse_ref, wide_ref, sem,
 ):
-    loads = []
-    for w in range(WALLS):
-        part = slice(w * LOCAL, (w + 1) * LOCAL)
-        loads.append(
-            pltpu.make_async_copy(inverse_hbm.at[part], inverse_ref.at[part], sems.at[w])
-        )
-        loads[-1].start()
     pairs = LOCAL // 2
+    load = pltpu.make_async_copy(inverse_hbm.at[:NY], inverse_ref, sem)
+    load.start()
 
     def gather(w):
         base = wall_base(w)
@@ -329,8 +325,7 @@
     def eliminate(w, got, before):
         got = got.reshape(pairs, PENS, ROWS, 2 * SLAB)
         if w == 0:
-            for load in loads:
-                load.wait()
+            load.wait()
         for i in range(pairs):
             planes = exchange_rows(got[i, :, :, :SLAB], got[i, :, :, SLAB:])
             for j, source in enumerate(planes):
@@ -375,7 +370,14 @@
                     out_ref[base + pen_offset(p), i, part] = value[part]
 
     high, low = fh[...], fl[...]
-    spectra = [span_dot(gather(w), high, low) for w in range(WALLS)]
+    def transform(step, carry):
+        for k in range(4):
+            w = step * 4 + k
+            wide_ref[w] = span_dot(gather(w), high, low)
+        return carry
+
+    lax.fori_loop(0, WALLS // 4, transform, 0)
+    spectra = wide_ref
     before = None
     for w in range(WALLS):
         before = eliminate(w, spectra[w], before)
@@ -421,7 +423,7 @@
         divisors,
         in_specs=[SMEM] * 4 + [VMEM],
         out_specs=HBM,
-        out_shape=jax.ShapeDtypeStruct((NY, PENS, ROWS, 128), F32),
+        out_shape=jax.ShapeDtypeStruct((SPARE * NY, PENS, ROWS, 128), F32),
         scratch_shapes=[pltpu.VMEM((NY, PENS, ROWS, 128), F32), pltpu.SemaphoreType.DMA(())],
         compiler_params=params(60),
         cost_estimate=pl.CostEstimate(flops=10**7, bytes_accessed=2 * MIB, transcendentals=0),
@@ -434,8 +436,11 @@
         out_specs=VMEM,
         out_shape=chunks,
         scratch_shapes=[pltpu.VMEM((NY, PENS, ROWS, 128), F32)] * 2
-        + [pltpu.SemaphoreType.DMA((WALLS,))],
-        compiler_params=params(48),
+        + [
+            pltpu.VMEM((WALLS, LOCAL // 2 * PENS * ROWS, 2 * SLAB), F32),
+            pltpu.SemaphoreType.DMA(()),
+        ],
+        compiler_params=params(40),
         name="span_solve",
     )(coef_table, stretch_index, spectra, inverse, *span_tables())
     solved = lax.all_to_all(solved, ORDER, 0, 0, tiled=True)

time: 87 us -> 85.9 us (0.987)
  Pallas kernels: 14.7 us -> 13.7 us
    pallas_call x1, Pallas kernels: 5.45 us -> 4.39 us  [on_device(): pl.pallas_call(span_solve, in_specs=[SMEM] * 2 + [VMEM, HBM] + [VMEM] * 6...]
where the time goes in v6:
time: 85.9 us; the launch traced here: 85.3 us
  blocking collectives  34.9 us (41%)
  waiting for transfers between devices  23.4 us (27%)
  Pallas kernels  13.7 us (16%)
  starting transfers between devices  11.5 us (13%)
  local copies, waits for them, and re-layouts  1.53 us (2%)
    all_to_all x1, blocking collectives, on_device(): solved = lax.all_to_all(solved, ORDER, 0, 0, tiled=True)  34.9 us
    all_to_all x1, waiting for transfers between devices, on_device(): spectra = lax.all_to_all(spectra, ORDER, 0, 0, tiled=True)  23.4 us
    all_to_all x1, starting transfers between devices, on_device(): spectra = lax.all_to_all(spectra, ORDER, 0, 0, tiled=True)  11.5 us
    pallas_call x1, Pallas kernels, on_device(): pl.pallas_call(span_solve, in_specs=[SMEM] * 2 + [VMEM, HBM] + [VMEM] * 6...  4.39 us
    pallas_call x1, Pallas kernels, on_device(): pl.pallas_call(stream_forward, in_specs=[HBM] * 2, out_specs=HBM, out_sha...  3.73 us
    pallas_call x1, Pallas kernels, on_device(): pl.pallas_call(divisors, in_specs=[SMEM] * 4 + [VMEM], out_specs=HBM, out...  3.64 us
    pallas_call x1, Pallas kernels, on_device(): pl.pallas_call(stream_backward, in_specs=[VMEM] * 2, out_specs=HBM, out_s...  1.98 us
  transfers between devices with their start and end apart: 1, of which 1 were waited for; matrix products, arithmetic and copies ran while one was open for 2% of the time, Pallas kernels for 4%

profile of v6, /device:TPU:1, one launch (start us, length us, event | category | flops | bytes accessed | tf_op | source)
XLA Modules:
  0.0 85.3 jit_solution(818319335308750329)
XLA Ops:
  0.0 3.7 %stream_forward.1 = f32[128,2,2,8,128]{4,3,2,1,0:T(8,128)} custom-call(f32[4,128,1024]{2,1,0:T(8,128)} %x_hbm.1, bf16[2048,256]{1,0:T(8,128)(2,1)} %constant.39.clone.table_hbm), custom_call_target="tpu_custom_call" | custom-call | tf_op jit(solution)/shard_map/stream_forward/pallas_call | solution.py:405
  3.7 0.0 copy-start.10
  3.7 0.0 copy-start.9
  3.8 11.5 %all-to-all-start = ((f32[128,2,2,8,128]{4,3,2,1,0:T(8,128)}), f32[128,2,2,8,128]{4,3,2,1,0:T(8,128)S(1)}, u32[]{:S(2)}, u32[]{:S(2)}) async-start(f32[128,2,2,8,128]{4,3,2,1,0:T(8,128)} %stream_forward.1), calls=%async_computation | async-start | bytes 4194304 | tf_op jit(solution)/shard_map/all_to_all | solution.py:432
  15.3 0.0 copy-done.10
  15.3 0.7 copy.18.table_ref
  16.0 0.0 copy-done.9
  16.0 0.1 reshape.7
  16.1 0.7 copy.16
  16.8 0.0 copy-start.5
  16.8 0.0 copy-start.6
  16.8 0.0 copy-start.7
  16.8 0.0 copy-start.8
  16.8 3.6 %divisors.1.inverse_hbm = f32[256,16,8,128]{3,2,1,0:T(8,128)} custom-call(s32[1]{0:T(128)} %bitcast.place_ref, f32[64,3]{1,0:T(8,128)} %copy.18.table_ref, s32[32]{0:T(128)} %level_ref.3, s32[512]{0:T(512)} %stream_ref.1, s32[16,128]{1,0:T(8,128)} %bitcast.2), custom_call_target="tpu_custom_call" | custom-call | flops 10000000 | bytes 2097152 | tf_op jit(solution)/shard_map/divisors/pallas_call | solution.py:422
  20.5 23.4 %all-to-all-done.in_ref = f32[128,2,2,8,128]{4,3,2,1,0:T(8,128)S(1)} async-done(((f32[128,2,2,8,128]{4,3,2,1,0:T(8,128)}), f32[128,2,2,8,128]{4,3,2,1,0:T(8,128)S(1)}, u32[]{:S(2)}, u32[]{:S(2)}) %all-to-all-start) | async-done | bytes 2097184 | tf_op jit(solution)/shard_map/all_to_all | solution.py:432
  43.9 0.0 copy-done.4
  43.9 0.0 copy-done.5
  43.9 0.0 copy-done.6
  43.9 0.0 copy-done.7
  43.9 0.0 copy-done.8
  43.9 4.4 %span_solve.1 = f32[128,2,2,8,128]{4,3,2,1,0:T(8,128)S(1)} custom-call(f32[64,3]{1,0:T(8,128)S(1)} %copy-done.1, s32[32]{0:T(128)S(1)} %copy-done.8, f32[128,2,2,8,128]{4,3,2,1,0:T(8,128)S(1)} %all-to-all-done.in_ref, f32[256,16,8,128]{3,2,1,0:T(8,128)} %divisors.1.inverse_hbm, bf16[256,256]{1,0:T(8,128)(2,1)S(1)} %copy-done.5, ...), custom_call_target="tpu_custom_call" | custom-call | tf_op jit(solution)/shard_map/span_solve/pallas_call | solution.py:433
  48.3 0.0 copy-start
  48.3 34.9 %all_to_all.10.y_ref = f32[128,2,2,8,128]{4,3,2,1,0:T(8,128)S(1)} all-to-all(f32[128,2,2,8,128]{4,3,2,1,0:T(8,128)S(1)} %span_solve.1), channel_id=1, replica_groups=mesh['x'=4,'core'=2,'z'=4,'y'=4] {'core','x','y','z'}, dimensions={0} | all-to-all | bytes 4194304 | tf_op jit(solution)/shard_map/all_to_all | solution.py:446
  83.3 2.0 %stream_backward.1 = f32[4,128,1024]{2,1,0:T(8,128)} custom-call(f32[128,2,2,8,128]{4,3,2,1,0:T(8,128)S(1)} %all_to_all.10.y_ref, bf16[2048,256]{1,0:T(8,128)(2,1)S(1)} %copy-done), custom_call_target="tpu_custom_call" | custom-call | tf_op jit(solution)/shard_map/stream_backward/pallas_call | solution.py:447
  (8 shorter events, 0.0 us)
Async XLA Ops:
  3.7 11.5 %copy-start.10 = (f32[64,3]{0,1:T(4,128)S(1)}, f32[64,3]{0,1:T(4,128)}, u32[]{:S(2)}) copy-start(f32[64,3]{0,1:T(4,128)} %param.14) | copy-start | bytes 2308
  3.7 12.3 %copy-start.9 = (s32[2048]{0:T(1024)S(1)}, s32[2048]{0:T(1024)}, u32[]{:S(2)}) copy-start(s32[2048]{0:T(1024)} %param.17) | copy-start | bytes 24580
  3.8 40.1 %all-to-all-start = ((f32[128,2,2,8,128]{4,3,2,1,0:T(8,128)}), f32[128,2,2,8,128]{4,3,2,1,0:T(8,128)S(1)}, u32[]{:S(2)}, u32[]{:S(2)}) async-start(f32[128,2,2,8,128]{4,3,2,1,0:T(8,128)} %stream_forward.1), calls=%async_computation | async-start | bytes 4194304 | tf_op jit(solution)/shard_map/all_to_all | solution.py:432
  16.8 27.1 %copy-start.1 = (f32[64,3]{1,0:T(8,128)S(1)}, f32[64,3]{1,0:T(8,128)}, u32[]{:S(2)}) copy-start(f32[64,3]{1,0:T(8,128)} %copy.18.table_ref) | copy-start | bytes 2308
  16.8 27.1 %copy-start.2 = (bf16[256,256]{1,0:T(8,128)(2,1)S(1)}, bf16[256,256]{1,0:T(8,128)(2,1)}, u32[]{:S(2)}) copy-start(bf16[256,256]{1,0:T(8,128)(2,1)} %constant.43.clone.bl) | copy-start | bytes 393220
  16.8 27.1 %copy-start.3 = (bf16[256,256]{1,0:T(8,128)(2,1)S(1)}, bf16[256,256]{1,0:T(8,128)(2,1)}, u32[]{:S(2)}) copy-start(bf16[256,256]{1,0:T(8,128)(2,1)} %constant.42.clone.bh) | copy-start | bytes 393220
  16.8 27.1 %copy-start.4 = (bf16[256,256]{1,0:T(8,128)(2,1)S(1)}, bf16[256,256]{1,0:T(8,128)(2,1)}, u32[]{:S(2)}) copy-start(bf16[256,256]{1,0:T(8,128)(2,1)} %constant.41.clone.fl) | copy-start | bytes 393220
  16.8 27.1 %copy-start.5 = (bf16[256,256]{1,0:T(8,128)(2,1)S(1)}, bf16[256,256]{1,0:T(8,128)(2,1)}, u32[]{:S(2)}) copy-start(bf16[256,256]{1,0:T(8,128)(2,1)} %constant.40.clone.fh) | copy-start | bytes 393220
  16.8 27.1 %copy-start.6 = (f32[16,8,128]{2,1,0:T(8,128)S(1)}, f32[16,8,128]{2,1,0:T(8,128)}, u32[]{:S(2)}) copy-start(f32[16,8,128]{2,1,0:T(8,128)} %constant.45.clone.sin_ref) | copy-start | bytes 196612
  16.8 27.1 %copy-start.7 = (f32[16,8,128]{2,1,0:T(8,128)S(1)}, f32[16,8,128]{2,1,0:T(8,128)}, u32[]{:S(2)}) copy-start(f32[16,8,128]{2,1,0:T(8,128)} %constant.44.clone.cos_ref) | copy-start | bytes 196612
  16.8 27.1 %copy-start.8 = (s32[32]{0:T(128)S(1)}, s32[32]{0:T(128)}, u32[]{:S(2)}) copy-start(s32[32]{0:T(128)} %level_ref.3) | copy-start | bytes 388
  48.3 35.0 %copy-start = (bf16[2048,256]{1,0:T(8,128)(2,1)S(1)}, bf16[2048,256]{1,0:T(8,128)(2,1)}, u32[]{:S(2)}) copy-start(bf16[2048,256]{1,0:T(8,128)(2,1)} %constant.46.clone.table_ref) | copy-start | bytes 3145732

commit v7 on v6

--- a/solution.py
+++ b/solution.py
@@ -17,8 +17,10 @@
 SLAB = NZ // PENS
 ROWS = 2 * OWN
 CLASSES = 4
+UNROLL = 4
 SPAN = KX // 2
 OWNERS = DEVICES // CLASSES
+STORES = (((0, 1, 2, 3),), ((0, 1), (2, 3)))
 SPARE = 8
 ROOT = np.float32(np.sqrt(0.5))
 MIB = 1 << 20
@@ -159,7 +161,7 @@
     for i in range(pairs):
         x_loads[i].wait()
         folded = fold(x_ref[2 * i : 2 * i + 2].reshape(2 * SLAB, NX))
-        for members in (((0,1,2,3),),((0,1),(2,3)))[i]:
+        for members in STORES[i]:
             for group in members:
                 high, low = split(folded[group])
                 start = 2 * SPAN * group
@@ -169,9 +171,8 @@
                     + dot(table, low)
                     + dot(table_ref[start + SPAN : start + 2 * SPAN], high)
                 )
-                parts = exchange_rows(
-                    *(got[:, j * SLAB : (j + 1) * SLAB].reshape(OWNERS, ROWS, SLAB) for j in (0, 1))
-                )
+                planes = (got[:, j * SLAB : (j + 1) * SLAB] for j in (0, 1))
+                parts = exchange_rows(*(p.reshape(OWNERS, ROWS, SLAB) for p in planes))
                 base = group * OWNERS
                 for k in (0, 1):
                     out_ref[base : base + OWNERS, i, k] = parts[k]
@@ -322,10 +323,8 @@
             jnp.concatenate([jnp.concatenate(real, 0), jnp.concatenate(imag, 0)], 1)
         )
 
-    def eliminate(w, got, before):
-        got = got.reshape(pairs, PENS, ROWS, 2 * SLAB)
-        if w == 0:
-            load.wait()
+    def eliminate(w, before):
+        got = wide_ref[w].reshape(pairs, PENS, ROWS, 2 * SLAB)
         for i in range(pairs):
             planes = exchange_rows(got[i, :, :, :SLAB], got[i, :, :, SLAB:])
             for j, source in enumerate(planes):
@@ -343,9 +342,8 @@
             for j in (1, 0):
                 plane = w * LOCAL + 2 * i + j
                 value = held_ref[plane]
-                if plane < NY - 1:
-                    upper = table_ref[level_ref[plane], 1]
-                    value = value - upper * inverse_ref[plane] * after
+                upper = table_ref[level_ref[plane], 1]
+                value = value - upper * inverse_ref[plane] * after
                 planes[j] = after = value
             re, im = exchange_rows(*planes)
             real.insert(0, re.reshape(PENS * ROWS, SLAB))
@@ -370,24 +368,28 @@
                     out_ref[base + pen_offset(p), i, part] = value[part]
 
     high, low = fh[...], fl[...]
-    def transform(step, carry):
-        for k in range(4):
-            w = step * 4 + k
+
+    def forward(step, carry):
+        for k in range(UNROLL):
+            w = step * UNROLL + k
             wide_ref[w] = span_dot(gather(w), high, low)
         return carry
 
-    lax.fori_loop(0, WALLS // 4, transform, 0)
-    spectra = wide_ref
+    lax.fori_loop(0, WALLS // UNROLL, forward, 0)
+    load.wait()
     before = None
     for w in range(WALLS):
-        before = eliminate(w, spectra[w], before)
+        before = eliminate(w, before)
     high, low = bh[...], bl[...]
-    after, parts = substitute(WALLS - 1, None)
-    for w in reversed(range(WALLS)):
-        got = span_dot(parts, high, low)
-        if w:
-            after, parts = substitute(w - 1, after)
-        scatter(w, got)
+
+    def backward(step, after):
+        for k in range(UNROLL):
+            w = WALLS - 1 - (step * UNROLL + k)
+            after, parts = substitute(w, after)
+            scatter(w, span_dot(parts, high, low))
+        return after
+
+    lax.fori_loop(0, WALLS // UNROLL, backward, jnp.zeros((PENS, ROWS, SLAB), F32))
 
 
 def params(mib):
@@ -413,7 +415,7 @@
             pltpu.VMEM(chunks.shape, F32),
             pltpu.SemaphoreType.DMA((LOCAL // 2,)),
             pltpu.SemaphoreType.DMA((CLASSES,)),
-            pltpu.SemaphoreType.DMA((LOCAL // 2 * CLASSES,)),
+            pltpu.SemaphoreType.DMA((sum(map(len, STORES)),)),
         ],
         compiler_params=params(60),
         name="stream_forward",

time: 85.9 us -> 85.9 us (level)
  no operation moved by 1% of the time
where the time goes in v7:
time: 85.9 us; the launch traced here: 85.3 us
  blocking collectives  34.9 us (41%)
  waiting for transfers between devices  23.4 us (27%)
  Pallas kernels  13.8 us (16%)
  starting transfers between devices  11.5 us (13%)
  local copies, waits for them, and re-layouts  1.53 us (2%)
    all_to_all x1, blocking collectives, on_device(): solved = lax.all_to_all(solved, ORDER, 0, 0, tiled=True)  34.9 us
    all_to_all x1, waiting for transfers between devices, on_device(): spectra = lax.all_to_all(spectra, ORDER, 0, 0, tiled=True)  23.4 us
    all_to_all x1, starting transfers between devices, on_device(): spectra = lax.all_to_all(spectra, ORDER, 0, 0, tiled=True)  11.5 us
    pallas_call x1, Pallas kernels, on_device(): pl.pallas_call(span_solve, in_specs=[SMEM] * 2 + [VMEM, HBM] + [VMEM] * 6...  4.51 us
    pallas_call x1, Pallas kernels, on_device(): pl.pallas_call(stream_forward, in_specs=[HBM] * 2, out_specs=HBM, out_sha...  3.68 us
    pallas_call x1, Pallas kernels, on_device(): pl.pallas_call(divisors, in_specs=[SMEM] * 4 + [VMEM], out_specs=HBM, out...  3.64 us
    pallas_call x1, Pallas kernels, on_device(): pl.pallas_call(stream_backward, in_specs=[VMEM] * 2, out_specs=HBM, out_s...  1.98 us
  transfers between devices with their start and end apart: 1, of which 1 were waited for; matrix products, arithmetic and copies ran while one was open for 2% of the time, Pallas kernels for 4%

profile of v7, /device:TPU:1, one launch (start us, length us, event | category | flops | bytes accessed | tf_op | source)
XLA Modules:
  0.0 85.3 jit_solution(11826556301302252190)
XLA Ops:
  0.0 3.7 %stream_forward.1 = f32[128,2,2,8,128]{4,3,2,1,0:T(8,128)} custom-call(f32[4,128,1024]{2,1,0:T(8,128)} %x_hbm.1, bf16[2048,256]{1,0:T(8,128)(2,1)} %constant.39.clone.table_hbm), custom_call_target="tpu_custom_call" | custom-call | tf_op jit(solution)/shard_map/stream_forward/pallas_call | solution.py:407
  3.7 0.0 copy-start.10
  3.7 0.0 copy-start.9
  3.7 11.5 %all-to-all-start = ((f32[128,2,2,8,128]{4,3,2,1,0:T(8,128)}), f32[128,2,2,8,128]{4,3,2,1,0:T(8,128)S(1)}, u32[]{:S(2)}, u32[]{:S(2)}) async-start(f32[128,2,2,8,128]{4,3,2,1,0:T(8,128)} %stream_forward.1), calls=%async_computation | async-start | bytes 4194304 | tf_op jit(solution)/shard_map/all_to_all | solution.py:434
  15.2 0.0 copy-done.10
  15.2 0.7 copy.18.table_ref
  16.0 0.0 copy-done.9
  16.0 0.1 reshape.7
  16.0 0.7 copy.16
  16.7 0.0 copy-start.5
  16.7 0.0 copy-start.6
  16.8 0.0 copy-start.7
  16.8 0.0 copy-start.8
  16.8 3.6 %divisors.1.inverse_hbm = f32[256,16,8,128]{3,2,1,0:T(8,128)} custom-call(s32[1]{0:T(128)} %bitcast.place_ref, f32[64,3]{1,0:T(8,128)} %copy.18.table_ref, s32[32]{0:T(128)} %level_ref.3, s32[512]{0:T(512)} %stream_ref.1, s32[16,128]{1,0:T(8,128)} %bitcast.2), custom_call_target="tpu_custom_call" | custom-call | flops 10000000 | bytes 2097152 | tf_op jit(solution)/shard_map/divisors/pallas_call | solution.py:424
  20.4 23.4 %all-to-all-done.in_ref = f32[128,2,2,8,128]{4,3,2,1,0:T(8,128)S(1)} async-done(((f32[128,2,2,8,128]{4,3,2,1,0:T(8,128)}), f32[128,2,2,8,128]{4,3,2,1,0:T(8,128)S(1)}, u32[]{:S(2)}, u32[]{:S(2)}) %all-to-all-start) | async-done | bytes 2097184 | tf_op jit(solution)/shard_map/all_to_all | solution.py:434
  43.8 0.0 copy-done.1
  43.8 0.0 copy-done.2
  43.8 0.0 copy-done.3
  43.8 0.0 copy-done.4
  43.9 4.5 %span_solve.1 = f32[128,2,2,8,128]{4,3,2,1,0:T(8,128)S(1)} custom-call(f32[64,3]{1,0:T(8,128)S(1)} %copy-done.1, s32[32]{0:T(128)S(1)} %copy-done.8, f32[128,2,2,8,128]{4,3,2,1,0:T(8,128)S(1)} %all-to-all-done.in_ref, f32[256,16,8,128]{3,2,1,0:T(8,128)} %divisors.1.inverse_hbm, bf16[256,256]{1,0:T(8,128)(2,1)S(1)} %copy-done.5, ...), custom_call_target="tpu_custom_call" | custom-call | tf_op jit(solution)/shard_map/span_solve/pallas_call | solution.py:435
  48.4 0.0 copy-start
  48.4 34.9 %all_to_all.10.y_ref = f32[128,2,2,8,128]{4,3,2,1,0:T(8,128)S(1)} all-to-all(f32[128,2,2,8,128]{4,3,2,1,0:T(8,128)S(1)} %span_solve.1), channel_id=1, replica_groups=mesh['x'=4,'core'=2,'z'=4,'y'=4] {'core','x','y','z'}, dimensions={0} | all-to-all | bytes 4194304 | tf_op jit(solution)/shard_map/all_to_all | solution.py:448
  83.4 0.0 copy-done
  83.4 2.0 %stream_backward.1 = f32[4,128,1024]{2,1,0:T(8,128)} custom-call(f32[128,2,2,8,128]{4,3,2,1,0:T(8,128)S(1)} %all_to_all.10.y_ref, bf16[2048,256]{1,0:T(8,128)(2,1)S(1)} %copy-done), custom_call_target="tpu_custom_call" | custom-call | tf_op jit(solution)/shard_map/stream_backward/pallas_call | solution.py:449
  (8 shorter events, 0.0 us)
Async XLA Ops:
  3.7 11.5 %copy-start.10 = (f32[64,3]{0,1:T(4,128)S(1)}, f32[64,3]{0,1:T(4,128)}, u32[]{:S(2)}) copy-start(f32[64,3]{0,1:T(4,128)} %param.14) | copy-start | bytes 2308
  3.7 12.3 %copy-start.9 = (s32[2048]{0:T(1024)S(1)}, s32[2048]{0:T(1024)}, u32[]{:S(2)}) copy-start(s32[2048]{0:T(1024)} %param.17) | copy-start | bytes 24580
  3.7 40.1 %all-to-all-start = ((f32[128,2,2,8,128]{4,3,2,1,0:T(8,128)}), f32[128,2,2,8,128]{4,3,2,1,0:T(8,128)S(1)}, u32[]{:S(2)}, u32[]{:S(2)}) async-start(f32[128,2,2,8,128]{4,3,2,1,0:T(8,128)} %stream_forward.1), calls=%async_computation | async-start | bytes 4194304 | tf_op jit(solution)/shard_map/all_to_all | solution.py:434
  16.7 27.1 %copy-start.1 = (f32[64,3]{1,0:T(8,128)S(1)}, f32[64,3]{1,0:T(8,128)}, u32[]{:S(2)}) copy-start(f32[64,3]{1,0:T(8,128)} %copy.18.table_ref) | copy-start | bytes 2308
  16.7 27.1 %copy-start.2 = (bf16[256,256]{1,0:T(8,128)(2,1)S(1)}, bf16[256,256]{1,0:T(8,128)(2,1)}, u32[]{:S(2)}) copy-start(bf16[256,256]{1,0:T(8,128)(2,1)} %constant.43.clone.bl) | copy-start | bytes 393220
  16.7 27.1 %copy-start.3 = (bf16[256,256]{1,0:T(8,128)(2,1)S(1)}, bf16[256,256]{1,0:T(8,128)(2,1)}, u32[]{:S(2)}) copy-start(bf16[256,256]{1,0:T(8,128)(2,1)} %constant.42.clone.bh) | copy-start | bytes 393220
  16.7 27.1 %copy-start.4 = (bf16[256,256]{1,0:T(8,128)(2,1)S(1)}, bf16[256,256]{1,0:T(8,128)(2,1)}, u32[]{:S(2)}) copy-start(bf16[256,256]{1,0:T(8,128)(2,1)} %constant.41.clone.fl) | copy-start | bytes 393220
  16.7 27.1 %copy-start.5 = (bf16[256,256]{1,0:T(8,128)(2,1)S(1)}, bf16[256,256]{1,0:T(8,128)(2,1)}, u32[]{:S(2)}) copy-start(bf16[256,256]{1,0:T(8,128)(2,1)} %constant.40.clone.fh) | copy-start | bytes 393220
  16.7 27.1 %copy-start.6 = (f32[16,8,128]{2,1,0:T(8,128)S(1)}, f32[16,8,128]{2,1,0:T(8,128)}, u32[]{:S(2)}) copy-start(f32[16,8,128]{2,1,0:T(8,128)} %constant.45.clone.sin_ref) | copy-start | bytes 196612
  16.8 27.1 %copy-start.7 = (f32[16,8,128]{2,1,0:T(8,128)S(1)}, f32[16,8,128]{2,1,0:T(8,128)}, u32[]{:S(2)}) copy-start(f32[16,8,128]{2,1,0:T(8,128)} %constant.44.clone.cos_ref) | copy-start | bytes 196612
  16.8 27.1 %copy-start.8 = (s32[32]{0:T(128)S(1)}, s32[32]{0:T(128)}, u32[]{:S(2)}) copy-start(s32[32]{0:T(128)} %level_ref.3) | copy-start | bytes 388
  48.4 35.0 %copy-start = (bf16[2048,256]{1,0:T(8,128)(2,1)S(1)}, bf16[2048,256]{1,0:T(8,128)(2,1)}, u32[]{:S(2)}) copy-start(bf16[2048,256]{1,0:T(8,128)(2,1)} %constant.46.clone.table_ref) | copy-start | bytes 3145732

commit v8 on v7

--- a/solution.py
+++ b/solution.py
@@ -26,7 +26,7 @@
 MIB = 1 << 20
 F32, BF16 = jnp.float32, jnp.bfloat16
 
-ORDER = ("core", "x", "y", "z")
+ORDER = ("core", "z", "y", "x")
 SIZES = {"x": 4, "core": 2, "z": 4, "y": 4}
 
 

time: 85.9 us -> 85.2 us (level)
  no operation moved by 1% of the time
where the time goes in v8:
time: 85.2 us; the launch traced here: 84.9 us
  blocking collectives  34.5 us (40%)
  waiting for transfers between devices  23.4 us (27%)
  Pallas kernels  13.8 us (16%)
  starting transfers between devices  11.5 us (13%)
  local copies, waits for them, and re-layouts  1.53 us (2%)
    all_to_all x1, blocking collectives, on_device(): solved = lax.all_to_all(solved, ORDER, 0, 0, tiled=True)  34.5 us
    all_to_all x1, waiting for transfers between devices, on_device(): spectra = lax.all_to_all(spectra, ORDER, 0, 0, tiled=True)  23.4 us
    all_to_all x1, starting transfers between devices, on_device(): spectra = lax.all_to_all(spectra, ORDER, 0, 0, tiled=True)  11.5 us
    pallas_call x1, Pallas kernels, on_device(): pl.pallas_call(span_solve, in_specs=[SMEM] * 2 + [VMEM, HBM] + [VMEM] * 6...  4.52 us
    pallas_call x1, Pallas kernels, on_device(): pl.pallas_call(stream_forward, in_specs=[HBM] * 2, out_specs=HBM, out_sha...  3.68 us
    pallas_call x1, Pallas kernels, on_device(): pl.pallas_call(divisors, in_specs=[SMEM] * 4 + [VMEM], out_specs=HBM, out...  3.64 us
    pallas_call x1, Pallas kernels, on_device(): pl.pallas_call(stream_backward, in_specs=[VMEM] * 2, out_specs=HBM, out_s...  1.98 us
  transfers between devices with their start and end apart: 1, of which 1 were waited for; matrix products, arithmetic and copies ran while one was open for 2% of the time, Pallas kernels for 4%

profile of v8, /device:TPU:1, one launch (start us, length us, event | category | flops | bytes accessed | tf_op | source)
XLA Modules:
  0.0 84.9 jit_solution(18287386001583516623)
XLA Ops:
  0.0 3.7 %stream_forward.1 = f32[128,2,2,8,128]{4,3,2,1,0:T(8,128)} custom-call(f32[4,128,1024]{2,1,0:T(8,128)} %x_hbm.1, bf16[2048,256]{1,0:T(8,128)(2,1)} %constant.39.clone.table_hbm), custom_call_target="tpu_custom_call" | custom-call | tf_op jit(solution)/shard_map/stream_forward/pallas_call | solution.py:407
  3.7 0.0 copy-start.10
  3.7 0.0 copy-start.9
  3.7 11.5 %all-to-all-start = ((f32[128,2,2,8,128]{4,3,2,1,0:T(8,128)}), f32[128,2,2,8,128]{4,3,2,1,0:T(8,128)S(1)}, u32[]{:S(2)}, u32[]{:S(2)}) async-start(f32[128,2,2,8,128]{4,3,2,1,0:T(8,128)} %stream_forward.1), calls=%async_computation | async-start | bytes 4194304 | tf_op jit(solution)/shard_map/all_to_all | solution.py:434
  15.2 0.0 copy-done.10
  15.2 0.7 copy.18.table_ref
  16.0 0.0 copy-done.9
  16.0 0.1 reshape.7
  16.0 0.7 copy.16
  16.7 0.0 copy-start.5
  16.7 0.0 copy-start.6
  16.8 0.0 copy-start.7
  16.8 0.0 copy-start.8
  16.8 3.6 %divisors.1.inverse_hbm = f32[256,16,8,128]{3,2,1,0:T(8,128)} custom-call(s32[1]{0:T(128)} %bitcast.place_ref, f32[64,3]{1,0:T(8,128)} %copy.18.table_ref, s32[32]{0:T(128)} %level_ref.3, s32[512]{0:T(512)} %stream_ref.1, s32[16,128]{1,0:T(8,128)} %bitcast.2), custom_call_target="tpu_custom_call" | custom-call | flops 10000000 | bytes 2097152 | tf_op jit(solution)/shard_map/divisors/pallas_call | solution.py:424
  20.4 23.4 %all-to-all-done.in_ref = f32[128,2,2,8,128]{4,3,2,1,0:T(8,128)S(1)} async-done(((f32[128,2,2,8,128]{4,3,2,1,0:T(8,128)}), f32[128,2,2,8,128]{4,3,2,1,0:T(8,128)S(1)}, u32[]{:S(2)}, u32[]{:S(2)}) %all-to-all-start) | async-done | bytes 2097184 | tf_op jit(solution)/shard_map/all_to_all | solution.py:434
  43.8 0.0 copy-done.1
  43.8 0.0 copy-done.2
  43.8 0.0 copy-done.3
  43.8 0.0 copy-done.4
  43.8 0.0 copy-done.5
  43.9 4.5 %span_solve.1 = f32[128,2,2,8,128]{4,3,2,1,0:T(8,128)S(1)} custom-call(f32[64,3]{1,0:T(8,128)S(1)} %copy-done.1, s32[32]{0:T(128)S(1)} %copy-done.8, f32[128,2,2,8,128]{4,3,2,1,0:T(8,128)S(1)} %all-to-all-done.in_ref, f32[256,16,8,128]{3,2,1,0:T(8,128)} %divisors.1.inverse_hbm, bf16[256,256]{1,0:T(8,128)(2,1)S(1)} %copy-done.5, ...), custom_call_target="tpu_custom_call" | custom-call | tf_op jit(solution)/shard_map/span_solve/pallas_call | solution.py:435
  48.4 0.0 copy-start
  48.4 34.5 %all_to_all.10.y_ref = f32[128,2,2,8,128]{4,3,2,1,0:T(8,128)S(1)} all-to-all(f32[128,2,2,8,128]{4,3,2,1,0:T(8,128)S(1)} %span_solve.1), channel_id=1, replica_groups=mesh['x'=4,'core'=2,'z'=4,'y'=4] {'core','z','y','x'}, dimensions={0} | all-to-all | bytes 4194304 | tf_op jit(solution)/shard_map/all_to_all | solution.py:448
  82.9 2.0 %stream_backward.1 = f32[4,128,1024]{2,1,0:T(8,128)} custom-call(f32[128,2,2,8,128]{4,3,2,1,0:T(8,128)S(1)} %all_to_all.10.y_ref, bf16[2048,256]{1,0:T(8,128)(2,1)S(1)} %copy-done), custom_call_target="tpu_custom_call" | custom-call | tf_op jit(solution)/shard_map/stream_backward/pallas_call | solution.py:449
  (8 shorter events, 0.0 us)
Async XLA Ops:
  3.7 11.5 %copy-start.10 = (f32[64,3]{0,1:T(4,128)S(1)}, f32[64,3]{0,1:T(4,128)}, u32[]{:S(2)}) copy-start(f32[64,3]{0,1:T(4,128)} %param.14) | copy-start | bytes 2308
  3.7 12.3 %copy-start.9 = (s32[2048]{0:T(1024)S(1)}, s32[2048]{0:T(1024)}, u32[]{:S(2)}) copy-start(s32[2048]{0:T(1024)} %param.17) | copy-start | bytes 24580
  3.7 40.1 %all-to-all-start = ((f32[128,2,2,8,128]{4,3,2,1,0:T(8,128)}), f32[128,2,2,8,128]{4,3,2,1,0:T(8,128)S(1)}, u32[]{:S(2)}, u32[]{:S(2)}) async-start(f32[128,2,2,8,128]{4,3,2,1,0:T(8,128)} %stream_forward.1), calls=%async_computation | async-start | bytes 4194304 | tf_op jit(solution)/shard_map/all_to_all | solution.py:434
  16.7 27.1 %copy-start.1 = (f32[64,3]{1,0:T(8,128)S(1)}, f32[64,3]{1,0:T(8,128)}, u32[]{:S(2)}) copy-start(f32[64,3]{1,0:T(8,128)} %copy.18.table_ref) | copy-start | bytes 2308
  16.7 27.1 %copy-start.2 = (bf16[256,256]{1,0:T(8,128)(2,1)S(1)}, bf16[256,256]{1,0:T(8,128)(2,1)}, u32[]{:S(2)}) copy-start(bf16[256,256]{1,0:T(8,128)(2,1)} %constant.43.clone.bl) | copy-start | bytes 393220
  16.7 27.1 %copy-start.3 = (bf16[256,256]{1,0:T(8,128)(2,1)S(1)}, bf16[256,256]{1,0:T(8,128)(2,1)}, u32[]{:S(2)}) copy-start(bf16[256,256]{1,0:T(8,128)(2,1)} %constant.42.clone.bh) | copy-start | bytes 393220
  16.7 27.1 %copy-start.4 = (bf16[256,256]{1,0:T(8,128)(2,1)S(1)}, bf16[256,256]{1,0:T(8,128)(2,1)}, u32[]{:S(2)}) copy-start(bf16[256,256]{1,0:T(8,128)(2,1)} %constant.41.clone.fl) | copy-start | bytes 393220
  16.7 27.1 %copy-start.5 = (bf16[256,256]{1,0:T(8,128)(2,1)S(1)}, bf16[256,256]{1,0:T(8,128)(2,1)}, u32[]{:S(2)}) copy-start(bf16[256,256]{1,0:T(8,128)(2,1)} %constant.40.clone.fh) | copy-start | bytes 393220
  16.7 27.1 %copy-start.6 = (f32[16,8,128]{2,1,0:T(8,128)S(1)}, f32[16,8,128]{2,1,0:T(8,128)}, u32[]{:S(2)}) copy-start(f32[16,8,128]{2,1,0:T(8,128)} %constant.45.clone.sin_ref) | copy-start | bytes 196612
  16.8 27.1 %copy-start.7 = (f32[16,8,128]{2,1,0:T(8,128)S(1)}, f32[16,8,128]{2,1,0:T(8,128)}, u32[]{:S(2)}) copy-start(f32[16,8,128]{2,1,0:T(8,128)} %constant.44.clone.cos_ref) | copy-start | bytes 196612
  16.8 27.1 %copy-start.8 = (s32[32]{0:T(128)S(1)}, s32[32]{0:T(128)}, u32[]{:S(2)}) copy-start(s32[32]{0:T(128)} %level_ref.3) | copy-start | bytes 388
  48.4 34.5 %copy-start = (bf16[2048,256]{1,0:T(8,128)(2,1)S(1)}, bf16[2048,256]{1,0:T(8,128)(2,1)}, u32[]{:S(2)}) copy-start(bf16[2048,256]{1,0:T(8,128)(2,1)} %constant.46.clone.table_ref) | copy-start | bytes 3145732

commit v9 on v6

--- a/solution.py
+++ b/solution.py
@@ -24,7 +24,7 @@
 MIB = 1 << 20
 F32, BF16 = jnp.float32, jnp.bfloat16
 
-ORDER = ("core", "x", "y", "z")
+ORDER = ("core", "z", "y", "x")
 SIZES = {"x": 4, "core": 2, "z": 4, "y": 4}
 
 

time: 85.9 us -> 85.1 us (level)
  no operation moved by 1% of the time
where the time goes in v9:
time: 85.1 us; the launch traced here: 84.8 us
  blocking collectives  34.5 us (41%)
  waiting for transfers between devices  23.4 us (27%)
  Pallas kernels  13.7 us (16%)
  starting transfers between devices  11.5 us (14%)
  local copies, waits for them, and re-layouts  1.53 us (2%)
    all_to_all x1, blocking collectives, on_device(): solved = lax.all_to_all(solved, ORDER, 0, 0, tiled=True)  34.5 us
    all_to_all x1, waiting for transfers between devices, on_device(): spectra = lax.all_to_all(spectra, ORDER, 0, 0, tiled=True)  23.4 us
    all_to_all x1, starting transfers between devices, on_device(): spectra = lax.all_to_all(spectra, ORDER, 0, 0, tiled=True)  11.5 us
    pallas_call x1, Pallas kernels, on_device(): pl.pallas_call(span_solve, in_specs=[SMEM] * 2 + [VMEM, HBM] + [VMEM] * 6...  4.39 us
    pallas_call x1, Pallas kernels, on_device(): pl.pallas_call(stream_forward, in_specs=[HBM] * 2, out_specs=HBM, out_sha...  3.73 us
    pallas_call x1, Pallas kernels, on_device(): pl.pallas_call(divisors, in_specs=[SMEM] * 4 + [VMEM], out_specs=HBM, out...  3.64 us
    pallas_call x1, Pallas kernels, on_device(): pl.pallas_call(stream_backward, in_specs=[VMEM] * 2, out_specs=HBM, out_s...  1.98 us
  transfers between devices with their start and end apart: 1, of which 1 were waited for; matrix products, arithmetic and copies ran while one was open for 2% of the time, Pallas kernels for 4%

profile of v9, /device:TPU:1, one launch (start us, length us, event | category | flops | bytes accessed | tf_op | source)
XLA Modules:
  0.0 84.8 jit_solution(14583319411555796303)
XLA Ops:
  0.0 3.7 %stream_forward.1 = f32[128,2,2,8,128]{4,3,2,1,0:T(8,128)} custom-call(f32[4,128,1024]{2,1,0:T(8,128)} %x_hbm.1, bf16[2048,256]{1,0:T(8,128)(2,1)} %constant.39.clone.table_hbm), custom_call_target="tpu_custom_call" | custom-call | tf_op jit(solution)/shard_map/stream_forward/pallas_call | solution.py:405
  3.7 0.0 copy-start.10
  3.7 0.0 copy-start.9
  3.8 11.5 %all-to-all-start = ((f32[128,2,2,8,128]{4,3,2,1,0:T(8,128)}), f32[128,2,2,8,128]{4,3,2,1,0:T(8,128)S(1)}, u32[]{:S(2)}, u32[]{:S(2)}) async-start(f32[128,2,2,8,128]{4,3,2,1,0:T(8,128)} %stream_forward.1), calls=%async_computation | async-start | bytes 4194304 | tf_op jit(solution)/shard_map/all_to_all | solution.py:432
  15.3 0.0 copy-done.10
  15.3 0.7 copy.18.table_ref
  16.0 0.1 reshape.7
  16.1 0.7 copy.16
  16.8 0.0 copy-start.5
  16.8 0.0 copy-start.6
  16.8 0.0 copy-start.7
  16.8 0.0 copy-start.8
  16.8 3.6 %divisors.1.inverse_hbm = f32[256,16,8,128]{3,2,1,0:T(8,128)} custom-call(s32[1]{0:T(128)} %bitcast.place_ref, f32[64,3]{1,0:T(8,128)} %copy.18.table_ref, s32[32]{0:T(128)} %level_ref.3, s32[512]{0:T(512)} %stream_ref.1, s32[16,128]{1,0:T(8,128)} %bitcast.2), custom_call_target="tpu_custom_call" | custom-call | flops 10000000 | bytes 2097152 | tf_op jit(solution)/shard_map/divisors/pallas_call | solution.py:422
  20.5 23.4 %all-to-all-done.in_ref = f32[128,2,2,8,128]{4,3,2,1,0:T(8,128)S(1)} async-done(((f32[128,2,2,8,128]{4,3,2,1,0:T(8,128)}), f32[128,2,2,8,128]{4,3,2,1,0:T(8,128)S(1)}, u32[]{:S(2)}, u32[]{:S(2)}) %all-to-all-start) | async-done | bytes 2097184 | tf_op jit(solution)/shard_map/all_to_all | solution.py:432
  43.9 0.0 copy-done.4
  43.9 0.0 copy-done.5
  43.9 0.0 copy-done.6
  43.9 0.0 copy-done.7
  43.9 0.0 copy-done.8
  43.9 4.4 %span_solve.1 = f32[128,2,2,8,128]{4,3,2,1,0:T(8,128)S(1)} custom-call(f32[64,3]{1,0:T(8,128)S(1)} %copy-done.1, s32[32]{0:T(128)S(1)} %copy-done.8, f32[128,2,2,8,128]{4,3,2,1,0:T(8,128)S(1)} %all-to-all-done.in_ref, f32[256,16,8,128]{3,2,1,0:T(8,128)} %divisors.1.inverse_hbm, bf16[256,256]{1,0:T(8,128)(2,1)S(1)} %copy-done.5, ...), custom_call_target="tpu_custom_call" | custom-call | tf_op jit(solution)/shard_map/span_solve/pallas_call | solution.py:433
  48.3 0.0 copy-start
  48.3 34.5 %all_to_all.10.y_ref = f32[128,2,2,8,128]{4,3,2,1,0:T(8,128)S(1)} all-to-all(f32[128,2,2,8,128]{4,3,2,1,0:T(8,128)S(1)} %span_solve.1), channel_id=1, replica_groups=mesh['x'=4,'core'=2,'z'=4,'y'=4] {'core','z','y','x'}, dimensions={0} | all-to-all | bytes 4194304 | tf_op jit(solution)/shard_map/all_to_all | solution.py:446
  82.8 0.0 copy-done
  82.8 2.0 %stream_backward.1 = f32[4,128,1024]{2,1,0:T(8,128)} custom-call(f32[128,2,2,8,128]{4,3,2,1,0:T(8,128)S(1)} %all_to_all.10.y_ref, bf16[2048,256]{1,0:T(8,128)(2,1)S(1)} %copy-done), custom_call_target="tpu_custom_call" | custom-call | tf_op jit(solution)/shard_map/stream_backward/pallas_call | solution.py:447
  (8 shorter events, 0.0 us)
Async XLA Ops:
  3.7 11.5 %copy-start.10 = (f32[64,3]{0,1:T(4,128)S(1)}, f32[64,3]{0,1:T(4,128)}, u32[]{:S(2)}) copy-start(f32[64,3]{0,1:T(4,128)} %param.14) | copy-start | bytes 2308
  3.7 12.3 %copy-start.9 = (s32[2048]{0:T(1024)S(1)}, s32[2048]{0:T(1024)}, u32[]{:S(2)}) copy-start(s32[2048]{0:T(1024)} %param.17) | copy-start | bytes 24580
  3.8 40.1 %all-to-all-start = ((f32[128,2,2,8,128]{4,3,2,1,0:T(8,128)}), f32[128,2,2,8,128]{4,3,2,1,0:T(8,128)S(1)}, u32[]{:S(2)}, u32[]{:S(2)}) async-start(f32[128,2,2,8,128]{4,3,2,1,0:T(8,128)} %stream_forward.1), calls=%async_computation | async-start | bytes 4194304 | tf_op jit(solution)/shard_map/all_to_all | solution.py:432
  16.8 27.1 %copy-start.1 = (f32[64,3]{1,0:T(8,128)S(1)}, f32[64,3]{1,0:T(8,128)}, u32[]{:S(2)}) copy-start(f32[64,3]{1,0:T(8,128)} %copy.18.table_ref) | copy-start | bytes 2308
  16.8 27.1 %copy-start.2 = (bf16[256,256]{1,0:T(8,128)(2,1)S(1)}, bf16[256,256]{1,0:T(8,128)(2,1)}, u32[]{:S(2)}) copy-start(bf16[256,256]{1,0:T(8,128)(2,1)} %constant.43.clone.bl) | copy-start | bytes 393220
  16.8 27.1 %copy-start.3 = (bf16[256,256]{1,0:T(8,128)(2,1)S(1)}, bf16[256,256]{1,0:T(8,128)(2,1)}, u32[]{:S(2)}) copy-start(bf16[256,256]{1,0:T(8,128)(2,1)} %constant.42.clone.bh) | copy-start | bytes 393220
  16.8 27.1 %copy-start.4 = (bf16[256,256]{1,0:T(8,128)(2,1)S(1)}, bf16[256,256]{1,0:T(8,128)(2,1)}, u32[]{:S(2)}) copy-start(bf16[256,256]{1,0:T(8,128)(2,1)} %constant.41.clone.fl) | copy-start | bytes 393220
  16.8 27.1 %copy-start.5 = (bf16[256,256]{1,0:T(8,128)(2,1)S(1)}, bf16[256,256]{1,0:T(8,128)(2,1)}, u32[]{:S(2)}) copy-start(bf16[256,256]{1,0:T(8,128)(2,1)} %constant.40.clone.fh) | copy-start | bytes 393220
  16.8 27.1 %copy-start.6 = (f32[16,8,128]{2,1,0:T(8,128)S(1)}, f32[16,8,128]{2,1,0:T(8,128)}, u32[]{:S(2)}) copy-start(f32[16,8,128]{2,1,0:T(8,128)} %constant.45.clone.sin_ref) | copy-start | bytes 196612
  16.8 27.1 %copy-start.7 = (f32[16,8,128]{2,1,0:T(8,128)S(1)}, f32[16,8,128]{2,1,0:T(8,128)}, u32[]{:S(2)}) copy-start(f32[16,8,128]{2,1,0:T(8,128)} %constant.44.clone.cos_ref) | copy-start | bytes 196612
  16.8 27.1 %copy-start.8 = (s32[32]{0:T(128)S(1)}, s32[32]{0:T(128)}, u32[]{:S(2)}) copy-start(s32[32]{0:T(128)} %level_ref.3) | copy-start | bytes 388
  48.3 34.5 %copy-start = (bf16[2048,256]{1,0:T(8,128)(2,1)S(1)}, bf16[2048,256]{1,0:T(8,128)(2,1)}, u32[]{:S(2)}) copy-start(bf16[2048,256]{1,0:T(8,128)(2,1)} %constant.46.clone.table_ref) | copy-start | bytes 3145732
